TPU v7x, 32 devices: a whole 2x2x4 slice. The times are simulated.
32 devices in a mesh: dp: 32 (over z, y, x, core).
Axes of the slice: x: 2, y: 2, z: 4, core: 2. Of those that a mesh axis runs over, the one named last changes fastest.
Arguments:
- inputs: bfloat16 [32768, 1024], P('dp'), may hold values from -6 to 6
- seq_lengths: int32 [64, 4], P('dp'), may hold values from 1 to 256, 512 in all within a row
- qkv_weight: bfloat16 [1024, 3072], P('dp'), may hold values from -0.1875 to 0.1875
- out_weight: bfloat16 [1024, 1024], P('dp'), may hold values from -0.75 to 0.75
- up_weight: bfloat16 [1024, 4096], P('dp'), may hold values from -0.1875 to 0.1875
- down_weight: bfloat16 [4096, 1024], P('dp'), may hold values from -0.09375 to 0.09375
- query_bias: bfloat16 [1024], P('dp'), may hold values from -3 to 3
- value_bias: bfloat16 [1024], P('dp'), may hold values from -3 to 3
- out_bias: bfloat16 [1024], P('dp'), may hold values from -3 to 3
- up_bias: bfloat16 [4096], P('dp'), may hold values from -3 to 3
- down_bias: bfloat16 [1024], P('dp'), may hold values from -3 to 3
- first_gain: bfloat16 [1024], P('dp'), may hold values from 0.5 to 1.5
- first_shift: bfloat16 [1024], P('dp'), may hold values from -3 to 3
- second_gain: bfloat16 [1024], P('dp'), may hold values from 0.5 to 1.5
- second_shift: bfloat16 [1024], P('dp'), may hold values from -3 to 3
- grad_output: bfloat16 [32768, 1024], P('dp'), may hold values from -6 to 6
Outputs:
- output: bfloat16 [32768, 1024], P('dp')
- grad_inputs: bfloat16 [32768, 1024], P('dp')
- grad_qkv: float32 [1024, 3072], P('dp')
- grad_out: float32 [1024, 1024], P('dp')
- grad_up: float32 [1024, 4096], P('dp')
- grad_down: float32 [4096, 1024], P('dp')
- grad_query_bias: float32 [1024], P('dp')
- grad_value_bias: float32 [1024], P('dp')
- grad_out_bias: float32 [1024], P('dp')
- grad_up_bias: float32 [4096], P('dp')
- grad_down_bias: float32 [1024], P('dp')
- grad_first_gain: float32 [1024], P('dp')
- grad_first_shift: float32 [1024], P('dp')
- grad_second_gain: float32 [1024], P('dp')
- grad_second_shift: float32 [1024], P('dp')
Inputs may be any that keep to these rules, and one draw needn't show every extreme that they name: `seq_lengths`: each row lists the lengths of the 4 sequences packed in order into one block of 512 tokens; every row sums to 512 and its largest entry is exactly 256. Device d holds rows d * 2 to d * 2 + 1, one per micro-batch.
All inputs are finite; a program needn't handle non-finite values.
Results may differ from a plain program's by a relative error of at most 0.013.
Values may be sent and summed in bfloat16 or wider, within the bound.
A program may use at most 256 MiB of HBM per device.

v0:
```python
import jax
import jax.numpy as jnp
from jax import lax
from jax.sharding import PartitionSpec as P

HEADS = 16


epsilon = 1e-05


def norm_rows(values, norm_gain, norm_shift):
    center = values - jnp.mean(values, axis=-1, keepdims=True)
    variance = jnp.mean(center * center, axis=-1, keepdims=True)
    inverse = lax.rsqrt(variance + epsilon)
    scaled = center * inverse
    return (scaled * norm_gain + norm_shift, scaled, inverse)


def norm_back(gradient, scaled, inverse, norm_gain):
    weighted = gradient * norm_gain
    mean_grad = jnp.mean(weighted, axis=-1, keepdims=True)
    mean_prod = jnp.mean(weighted * scaled, axis=-1, keepdims=True)
    result = inverse * (weighted - mean_grad - scaled * mean_prod)
    return (result, jnp.sum(gradient * scaled, axis=0), jnp.sum(gradient, axis=0))


def allowed_pairs(lengths_row, row_count):
    seq_ends = jnp.cumsum(lengths_row)
    places = jnp.arange(row_count, dtype=jnp.int32)
    labels = jnp.sum((places[:, None] >= seq_ends[None, :]).astype(jnp.int32), axis=1)
    return labels[:, None] == labels[None, :]


def head_parts(mixed_low):
    row_count = mixed_low.shape[0]
    head_size = mixed_low.shape[1] // 3 // HEADS
    split = mixed_low.reshape(row_count, 3, HEADS, head_size)
    return (split[:, 0], split[:, 1], split[:, 2], head_size ** (-0.5))


def score_block(queries, keys_all, allowed, factor):
    scores = (
        jnp.einsum("qhd,khd->hqk", queries, keys_all, preferred_element_type=jnp.float32) * factor
    )
    return jnp.where(allowed[None], scores, -1e30)


def attend(mixed_low, allowed):
    queries, keys_all, values, factor = head_parts(mixed_low)
    scores = score_block(queries, keys_all, allowed, factor)
    top_score = jnp.max(scores, axis=-1, keepdims=True)
    expo = jnp.exp(scores - top_score)
    total = jnp.sum(expo, axis=-1, keepdims=True)
    probs = expo / total
    attended = jnp.einsum(
        "hqk,khd->qhd", probs.astype(jnp.bfloat16), values, preferred_element_type=jnp.float32
    )
    return (attended.reshape(mixed_low.shape[0], -1), top_score + jnp.log(total))


def attend_back(mixed_low, allowed, log_total, grad_attended):
    queries, keys_all, values, factor = head_parts(mixed_low)
    row_count = mixed_low.shape[0]
    probs = jnp.exp(score_block(queries, keys_all, allowed, factor) - log_total)
    grad_heads = grad_attended.reshape(row_count, HEADS, -1)
    grad_values = jnp.einsum(
        "hqk,qhd->khd", probs.astype(jnp.bfloat16), grad_heads, preferred_element_type=jnp.float32
    )
    grad_probs = jnp.einsum("qhd,khd->hqk", grad_heads, values, preferred_element_type=jnp.float32)
    grad_scores = probs * (grad_probs - jnp.sum(probs * grad_probs, axis=-1, keepdims=True))
    scores_low = grad_scores.astype(jnp.bfloat16)
    grad_queries = (
        jnp.einsum("hqk,khd->qhd", scores_low, keys_all, preferred_element_type=jnp.float32)
        * factor
    )
    grad_keys = (
        jnp.einsum("hqk,qhd->khd", scores_low, queries, preferred_element_type=jnp.float32) * factor
    )
    stacked = jnp.stack([grad_queries, grad_keys, grad_values], axis=1)
    return stacked.reshape(row_count, -1)


def forward_block(params, tokens, lengths_row):
    (
        whole_qkv,
        whole_out,
        whole_up,
        whole_down,
        bias_query,
        bias_value,
        bias_out,
        bias_up,
        bias_down,
        gain_first,
        shift_first,
        gain_second,
        shift_second,
    ) = params
    row_count = tokens.shape[0]
    allowed = allowed_pairs(lengths_row, row_count)
    bias_all = jnp.concatenate([bias_query, jnp.zeros_like(bias_query), bias_value]).astype(
        jnp.float32
    )
    mixed_low = (jnp.dot(tokens, whole_qkv, preferred_element_type=jnp.float32) + bias_all).astype(
        jnp.bfloat16
    )
    attended, log_total = attend(mixed_low, allowed)
    attended_low = attended.astype(jnp.bfloat16)
    branch = jnp.dot(attended_low, whole_out, preferred_element_type=jnp.float32) + bias_out.astype(
        jnp.float32
    )
    hidden, scaled_first, inverse_first = norm_rows(
        tokens.astype(jnp.float32) + branch,
        gain_first.astype(jnp.float32),
        shift_first.astype(jnp.float32),
    )
    hidden_low = hidden.astype(jnp.bfloat16)
    pre_act = jnp.dot(hidden_low, whole_up, preferred_element_type=jnp.float32) + bias_up.astype(
        jnp.float32
    )
    activ_low = jax.nn.gelu(pre_act, approximate=False).astype(jnp.bfloat16)
    second = jnp.dot(activ_low, whole_down, preferred_element_type=jnp.float32) + bias_down.astype(
        jnp.float32
    )
    result, scaled_second, inverse_second = norm_rows(
        hidden + second, gain_second.astype(jnp.float32), shift_second.astype(jnp.float32)
    )
    kept = (
        mixed_low,
        allowed,
        log_total,
        attended_low,
        scaled_first,
        inverse_first,
        hidden_low,
        pre_act,
        activ_low,
        scaled_second,
        inverse_second,
    )
    return (result.astype(jnp.bfloat16), kept)


def backward_block(params, tokens, kept, grad_rows):
    (
        whole_qkv,
        whole_out,
        whole_up,
        whole_down,
        bias_query,
        bias_value,
        bias_out,
        bias_up,
        bias_down,
        gain_first,
        shift_first,
        gain_second,
        shift_second,
    ) = params
    (
        mixed_low,
        allowed,
        log_total,
        attended_low,
        scaled_first,
        inverse_first,
        hidden_low,
        pre_act,
        activ_low,
        scaled_second,
        inverse_second,
    ) = kept
    width = tokens.shape[1]
    grad_second_in, grad_gain_two, grad_shift_two = norm_back(
        grad_rows.astype(jnp.float32),
        scaled_second,
        inverse_second,
        gain_second.astype(jnp.float32),
    )
    grad_branch_two = grad_second_in.astype(jnp.bfloat16)
    grad_down_bias = jnp.sum(grad_branch_two.astype(jnp.float32), axis=0)
    grad_down = jnp.einsum(
        "tf,td->fd", activ_low, grad_branch_two, preferred_element_type=jnp.float32
    )
    grad_activ = jnp.einsum(
        "td,fd->tf", grad_branch_two, whole_down, preferred_element_type=jnp.float32
    )
    gelu_value, gelu_back = jax.vjp(
        lambda argument: jax.nn.gelu(argument, approximate=False), pre_act
    )
    grad_pre_low = gelu_back(grad_activ)[0].astype(jnp.bfloat16)
    grad_up_bias = jnp.sum(grad_pre_low.astype(jnp.float32), axis=0)
    grad_up = jnp.einsum("td,tf->df", hidden_low, grad_pre_low, preferred_element_type=jnp.float32)
    grad_hidden = grad_second_in + jnp.einsum(
        "tf,df->td", grad_pre_low, whole_up, preferred_element_type=jnp.float32
    )
    grad_first_in, grad_gain_one, grad_shift_one = norm_back(
        grad_hidden, scaled_first, inverse_first, gain_first.astype(jnp.float32)
    )
    grad_branch_one = grad_first_in.astype(jnp.bfloat16)
    grad_out_bias = jnp.sum(grad_branch_one.astype(jnp.float32), axis=0)
    grad_out = jnp.einsum(
        "tc,td->cd", attended_low, grad_branch_one, preferred_element_type=jnp.float32
    )
    grad_attended = jnp.einsum(
        "td,cd->tc", grad_branch_one, whole_out, preferred_element_type=jnp.float32
    ).astype(jnp.bfloat16)
    grad_mixed = attend_back(mixed_low, allowed, log_total, grad_attended).astype(jnp.bfloat16)
    grad_mixed_wide = grad_mixed.astype(jnp.float32)
    grad_query_bias = jnp.sum(grad_mixed_wide[:, :width], axis=0)
    grad_value_bias = jnp.sum(grad_mixed_wide[:, 2 * width :], axis=0)
    grad_qkv = jnp.einsum("td,tc->dc", tokens, grad_mixed, preferred_element_type=jnp.float32)
    grad_tokens = grad_first_in + jnp.einsum(
        "tc,dc->td", grad_mixed, whole_qkv, preferred_element_type=jnp.float32
    )
    grads = (
        grad_qkv,
        grad_out,
        grad_up,
        grad_down,
        grad_query_bias,
        grad_value_bias,
        grad_out_bias,
        grad_up_bias,
        grad_down_bias,
        grad_gain_one,
        grad_shift_one,
        grad_gain_two,
        grad_shift_two,
    )
    return (grad_tokens.astype(jnp.bfloat16), grads)


def body(
    inputs,
    seq_lengths,
    qkv_weight,
    out_weight,
    up_weight,
    down_weight,
    query_bias,
    value_bias,
    out_bias,
    up_bias,
    down_bias,
    first_gain,
    first_shift,
    second_gain,
    second_shift,
    grad_output,
):
    micro_count = seq_lengths.shape[0]
    slot_rows = inputs.shape[0] // micro_count
    outputs_all = []
    grads_all = []
    totals = None
    for index_micro in range(micro_count):
        tokens = inputs[index_micro * slot_rows : (index_micro + 1) * slot_rows]
        grad_rows = grad_output[index_micro * slot_rows : (index_micro + 1) * slot_rows]
        params = (
            lax.all_gather(qkv_weight, "dp", axis=0, tiled=True),
            lax.all_gather(out_weight, "dp", axis=0, tiled=True),
            lax.all_gather(up_weight, "dp", axis=0, tiled=True),
            lax.all_gather(down_weight, "dp", axis=0, tiled=True),
            lax.all_gather(query_bias, "dp", axis=0, tiled=True),
            lax.all_gather(value_bias, "dp", axis=0, tiled=True),
            lax.all_gather(out_bias, "dp", axis=0, tiled=True),
            lax.all_gather(up_bias, "dp", axis=0, tiled=True),
            lax.all_gather(down_bias, "dp", axis=0, tiled=True),
            lax.all_gather(first_gain, "dp", axis=0, tiled=True),
            lax.all_gather(first_shift, "dp", axis=0, tiled=True),
            lax.all_gather(second_gain, "dp", axis=0, tiled=True),
            lax.all_gather(second_shift, "dp", axis=0, tiled=True),
        )
        result, kept = forward_block(params, tokens, seq_lengths[index_micro])
        params = (
            lax.all_gather(qkv_weight, "dp", axis=0, tiled=True),
            lax.all_gather(out_weight, "dp", axis=0, tiled=True),
            lax.all_gather(up_weight, "dp", axis=0, tiled=True),
            lax.all_gather(down_weight, "dp", axis=0, tiled=True),
            lax.all_gather(query_bias, "dp", axis=0, tiled=True),
            lax.all_gather(value_bias, "dp", axis=0, tiled=True),
            lax.all_gather(out_bias, "dp", axis=0, tiled=True),
            lax.all_gather(up_bias, "dp", axis=0, tiled=True),
            lax.all_gather(down_bias, "dp", axis=0, tiled=True),
            lax.all_gather(first_gain, "dp", axis=0, tiled=True),
            lax.all_gather(first_shift, "dp", axis=0, tiled=True),
            lax.all_gather(second_gain, "dp", axis=0, tiled=True),
            lax.all_gather(second_shift, "dp", axis=0, tiled=True),
        )
        grad_tokens, grads = backward_block(params, tokens, kept, grad_rows)
        if totals is None:
            totals = grads
        else:
            totals = tuple((earlier + latest for earlier, latest in zip(totals, grads)))
        outputs_all.append(result)
        grads_all.append(grad_tokens)
    (
        sum_qkv,
        sum_out,
        sum_up,
        sum_down,
        sum_query_bias,
        sum_value_bias,
        sum_out_bias,
        sum_up_bias,
        sum_down_bias,
        sum_gain_one,
        sum_shift_one,
        sum_gain_two,
        sum_shift_two,
    ) = totals
    shares = (
        lax.psum_scatter(sum_qkv, "dp", scatter_dimension=0, tiled=True),
        lax.psum_scatter(sum_out, "dp", scatter_dimension=0, tiled=True),
        lax.psum_scatter(sum_up, "dp", scatter_dimension=0, tiled=True),
        lax.psum_scatter(sum_down, "dp", scatter_dimension=0, tiled=True),
        lax.psum_scatter(sum_query_bias, "dp", scatter_dimension=0, tiled=True),
        lax.psum_scatter(sum_value_bias, "dp", scatter_dimension=0, tiled=True),
        lax.psum_scatter(sum_out_bias, "dp", scatter_dimension=0, tiled=True),
        lax.psum_scatter(sum_up_bias, "dp", scatter_dimension=0, tiled=True),
        lax.psum_scatter(sum_down_bias, "dp", scatter_dimension=0, tiled=True),
        lax.psum_scatter(sum_gain_one, "dp", scatter_dimension=0, tiled=True),
        lax.psum_scatter(sum_shift_one, "dp", scatter_dimension=0, tiled=True),
        lax.psum_scatter(sum_gain_two, "dp", scatter_dimension=0, tiled=True),
        lax.psum_scatter(sum_shift_two, "dp", scatter_dimension=0, tiled=True),
    )
    return (
        jnp.concatenate(outputs_all, axis=0),
        jnp.concatenate(grads_all, axis=0),
        shares[0],
        shares[1],
        shares[2],
        shares[3],
        shares[4],
        shares[5],
        shares[6],
        shares[7],
        shares[8],
        shares[9],
        shares[10],
        shares[11],
        shares[12],
    )


def solution(mesh):
    return jax.shard_map(
        body,
        mesh=mesh,
        in_specs=(
            P("dp", None),
            P("dp", None),
            P("dp", None),
            P("dp", None),
            P("dp", None),
            P("dp", None),
            P("dp"),
            P("dp"),
            P("dp"),
            P("dp"),
            P("dp"),
            P("dp"),
            P("dp"),
            P("dp"),
            P("dp"),
            P("dp", None),
        ),
        out_specs=(
            P("dp", None),
            P("dp", None),
            P("dp", None),
            P("dp", None),
            P("dp", None),
            P("dp", None),
            P("dp"),
            P("dp"),
            P("dp"),
            P("dp"),
            P("dp"),
            P("dp"),
            P("dp"),
            P("dp"),
            P("dp"),
        ),
        check_vma=False,
    )
```

profile of v0, /device:TPU:0, one launch (start us, length us, event | category | flops | bytes accessed | tf_op | source)
XLA Modules:
  0.0 1098.3 jit_solution(8178400328405845028)
XLA Ops:
  18.0 42.3 %all-reduce.18 = (bf16[1024]{0:T(1024)(128)(2,1)S(1)}, bf16[1024]{0:T(1024)(128)(2,1)S(1)}, bf16[1024]{0:T(1024)(128)(2,1)S(1)}, bf16[1024]{0:T(1024)(128)(2,1)S...) all-reduce(bf16[1024]{0:T(1024)(128)(2,1)S(1)} %dynamic-update-slic, ...), channel_id=1, replica_groups=mesh['dp'=32] {'dp'}, use_global_device_ids=true, to_apply=%add.1 | all-reduce | flops 8192 | bytes 32768
  62.1 40.8 %all-gather = bf16[32,1,128]{2,1,0:T(2,128)(2,1)S(1)} all-gather(bf16[1,1,128]{2,1,0:T(2,128)(2,1)} %bitcast.152), channel_id=1, replica_groups=mesh['dp'=32] {'dp'}, dimensions={0}, use_global_device_ids=true | all-gather | bytes 8448 | tf_op jit(solution)/shard_map/all_gather | solution.py:269
  104.1 8.2 add_convert_fusion.3
  115.7 8.4 fusion.92
  124.0 8.6 fusion
  133.2 8.7 fusion.41
  160.2 8.3 fusion.1
  169.1 8.7 fusion.40
  183.7 36.8 %all-gather.10.cloned.1.call-done = bf16[1024,4096]{1,0:T(8,128)(2,1)} async-done(((bf16[32,4096]{1,0:T(8,128)(2,1)}), bf16[1024,4096]{1,0:T(8,128)(2,1)}) %all-gather.10.cloned.1.call-update) | async-done | bytes 8388624 | tf_op jit(solution)/shard_map/all_gather | solution.py:264
  230.9 49.0 %multiply_convert_fusion.3 = (bf16[512,4096]{1,0:T(8,128)(2,1)}, f32[512,4096]{1,0:T(8,128)}, bf16[512,4096]{1,0:T(8,128)(2,1)}, f32[512,4096]{1,0:T(8,128)}, f32[512,4096]{1,0:T(8,128)}) fusion(f32[4096]{0:T(1024)S(1)} %bitcast.149, f32[512,4096]{1,0:T(8,128)S(1)} %fusion.82, bf16[1024,4096]{1,0:T(8,128)(2,1)S(1)} %copy-done.61, ...), kind=kOutput, calls=%fused_computation.42 | convolution fusion | flops 4574412800 | bytes 52457472 | tf_op jit(solution)/shard_map/dot_general | solution.py:119
  279.9 19.3 %all-gather.12.cloned.1.call-done = bf16[4096,1024]{1,0:T(8,128)(2,1)} async-done(((bf16[128,1024]{1,0:T(8,128)(2,1)}), bf16[4096,1024]{1,0:T(8,128)(2,1)}) %all-gather.12.cloned.1.call-update) | async-done | bytes 8388624 | tf_op jit(solution)/shard_map/all_gather | solution.py:265
  299.3 10.0 fusion.97
  321.5 16.9 %convert_reduce_fusion.1 = (f32[4096]{0:T(1024)}, bf16[512,4096]{1,0:T(8,128)(2,1)}) fusion(f32[512,4096]{1,0:T(8,128)} %get-tuple-element.129, bf16[4096,1024]{1,0:T(8,128)(2,1)} %all-gather.12.cloned.1.call-done, f32[512,1024]{1,0:T(8,128)} %get-tuple-element.136, f32[512,4096]{1,0:T(8,128)} %get-tuple-element.153, f32[4096]{0:T(1024)S(1)} %bitcast.150), kind=kOutput, calls=%fused_computation.24 | convolution fusion | flops 4331139072 | bytes 31490048 | tf_op jit(solution)/shard_map/td,fd->tf/dot_general | solution.py:186
  338.4 11.7 %multiply_reduce_fusion.3 = (f32[1024]{0:T(1024)}, f32[512]{0:T(512)S(1)}, f32[512]{0:T(512)S(1)}, f32[1024]{0:T(1024)}, f32[512,1024]{1,0:T(8,128)}) fusion(f32[512,1024]{1,0:T(8,128)S(1)} %copy-done.18, f32[512]{0:T(512)S(1)} %add_rsqrt_fusion.3, f32[512]{0:T(512)S(1)} %broadcast_multiply_fusion.11, f32[1024]{0:T(1024)S(1)} %convert_element_type.189, ...), kind=kOutput, calls=%fused_computation.93 | convolution fusion | flops 4300207104 | bytes 18894848 | tf_op jit(solution)/shard_map/tf,df->td/dot_general | solution.py:195
  350.1 15.5 %convert_reduce_fusion = (f32[4096]{0:T(1024)}, bf16[512,4096]{1,0:T(8,128)(2,1)}) fusion(f32[512,4096]{1,0:T(8,128)} %get-tuple-element.138, bf16[4096,1024]{1,0:T(8,128)(2,1)} %all-gather.12.cloned.1.call-done, f32[512,1024]{1,0:T(8,128)S(1)} %get-tuple-element.121, f32[512,4096]{1,0:T(8,128)} %copy-done.63, f32[4096]{0:T(1024)S(1)} %bitcast.151), kind=kOutput, calls=%fused_computation.23 | convolution fusion | flops 4331139072 | bytes 31490048 | tf_op jit(solution)/shard_map/td,fd->tf/dot_general | solution.py:186
  365.6 12.7 %convert_reduce_fusion.7 = (f32[1024]{0:T(1024)}, f32[512,1024]{1,0:T(8,128)S(1)}, f32[1024]{0:T(1024)}, f32[512]{0:T(512)S(1)}, f32[512]{0:T(512)S(1)}, /*index=5*/f32[1024]{0:T(1024)}, f32[512,1024]{1,0:T(8,128)}) fusion(f32[512]{0:T(512)S(1)} %broadcast_multiply_fusion.4, f32[512,1024]{1,0:T(8,128)S(1)} %copy-done.18, ...), kind=kOutput, calls=%fused_computation.97 | convolution fusion | flops 4305448960 | bytes 25198592 | tf_op jit(solution)/shard_map/tf,df->td/dot_general | solution.py:195
  385.4 11.3 %multiply_reduce_fusion.1 = (f32[16,512]{1,0:T(8,128)S(1)}, f32[16,512,512]{1,2,0:T(8,128)}) fusion(f32[16,512,512]{1,2,0:T(8,128)} %get-tuple-element.146, f32[16,512]{1,0:T(8,128)S(1)} %copy-done.37, bf16[512,16,64]{0,2,1:T(8,128)(2,1)S(1)} %bitcast.141, bf16[512,3,16,64]{0,3,2,1:T(8,128)(2,1)} %bitcast.135), kind=kOutput, calls=%fused_computation.4 | convolution fusion | flops 549445632 | bytes 35717120 | tf_op jit(solution)/shard_map/qhd,khd->hqk/dot_general | solution.py:70
  396.7 12.2 %multiply_convert_fusion.1 = bf16[16,512,512]{1,2,0:T(8,128)(2,1)S(1)} fusion(f32[16,512,512]{1,2,0:T(8,128)} %get-tuple-element.163, f32[16,512,512]{1,2,0:T(8,128)} %get-tuple-element.146, f32[16,512]{1,0:T(8,128)S(1)} %get-tuple-element.162, f32[16,512]{1,0:T(8,128)S(1)} %copy-done.37), kind=kLoop, calls=%fused_computation.3 | loop fusion | flops 16777216 | bytes 42008576 | tf_op jit(solution)/shard_map/convert_element_type | solution.py:72
  429.2 8.6 fusion.55
  441.2 10.9 multiply_reduce_fusion
  452.1 15.6 %multiply_convert_fusion = bf16[16,512,512]{1,2,0:T(8,128)(2,1)} fusion(f32[16,512,512]{1,2,0:T(8,128)} %get-tuple-element.161, f32[16,512,512]{1,2,0:T(8,128)} %get-tuple-element.150, f32[16,512]{1,0:T(8,128)S(1)} %get-tuple-element.160, f32[16,512]{1,0:T(8,128)S(1)} %copy-done.36), kind=kLoop, calls=%fused_computation | loop fusion | flops 16777216 | bytes 42008576 | tf_op jit(solution)/shard_map/convert_element_type | solution.py:72
  467.8 7.8 fusion.51
  499.6 12.6 %copy.97 = f32[1024,3072]{1,0:T(8,128)} copy(f32[1024,3072]{0,1:T(8,128)} %add_bitcast_fusion) | data formatting | bytes 25165824
  512.9 13.4 %fusion.84 = f32[1024,4096]{1,0:T(8,128)} fusion(bf16[512,4096]{1,0:T(8,128)(2,1)} %get-tuple-element.165, f32[512,1024]{1,0:T(8,128)} %copy-done.16, f32[1024]{0:T(1024)S(1)} %copy-done.39, f32[1024]{0:T(1024)S(1)} %convert_element_type.189, f32[512]{0:T(512)S(1)} %copy-done.60, f32[512]{0:T(512)S(1)} %copy-done.52), kind=kOutput, calls=%fused_computation.195 | convolution fusion | flops 4297588736 | bytes 23080960 | tf_op jit(solution)/shard_map/td,tf->df/dot_general | solution.py:194
  526.3 12.1 %convolution_add_fusion = f32[1024,4096]{1,0:T(8,128)} fusion(f32[1024,4096]{1,0:T(8,128)} %fusion.84, bf16[512,4096]{1,0:T(8,128)(2,1)S(1)} %copy-done.28, f32[512,1024]{1,0:T(8,128)S(1)} %copy-done.1, f32[512]{0:T(512)S(1)} %add_rsqrt_fusion.1, f32[512]{0:T(512)S(1)} %broadcast_multiply_fusion.9, f32[1024]{0:T(1024)S(1)} %copy-done.39, ...), kind=kOutput, calls=%fused_computation.59 | convolution fusion | flops 4301783040 | bytes 39858176 | tf_op jit(solution)/shard_map/td,tf->df/dot_general | solution.py:194
  538.4 13.3 %fusion.75 = f32[4096,1024]{1,0:T(8,128)} fusion(bf16[512,4096]{1,0:T(8,128)(2,1)} %get-tuple-element.128, f32[512,1024]{1,0:T(8,128)} %get-tuple-element.136), kind=kOutput, calls=%fused_computation.190 | convolution fusion | flops 4295491584 | bytes 23068672 | tf_op jit(solution)/shard_map/tf,td->fd/dot_general | solution.py:183
  551.7 11.7 %convolution_add_fusion.1 = f32[4096,1024]{1,0:T(8,128)} fusion(f32[4096,1024]{1,0:T(8,128)} %fusion.75, bf16[512,4096]{1,0:T(8,128)(2,1)S(1)} %copy-done.12, f32[512,1024]{1,0:T(8,128)S(1)} %copy-done.22), kind=kOutput, calls=%fused_computation.62 | convolution fusion | flops 4299685888 | bytes 39845888 | tf_op jit(solution)/shard_map/tf,td->fd/dot_general | solution.py:183
  568.2 40.2 %all-reduce.17 = (f32[1024]{0:T(1024)S(1)}, f32[1024]{0:T(1024)S(1)}, f32[1024]{0:T(1024)S(1)}, f32[4096]{0:T(1024)S(1)}, f32[1024]{0:T(1024)S(1)}, /*index=5*/f...) all-reduce(f32[1024]{0:T(1024)S(1)} %add.261, ...), channel_id=6, replica_groups=mesh['dp'=32] {'dp'}, use_global_device_ids=true, to_apply=%region_32.33.clone | all-reduce | flops 12288 | bytes 98304
  616.8 8.0 add_convert_fusion.5
  632.5 86.4 %reduce-scatter.13.cloned.1.call-done = f32[32,3072]{1,0:T(8,128)} async-done(((f32[1024,3072]{1,0:T(8,128)}), f32[32,3072]{1,0:T(8,128)}) %reduce-scatter.13.cloned.1.call-update) | async-done | bytes 393232
  718.9 184.8 %reduce-scatter.9.cloned.1.call-done = f32[32,4096]{1,0:T(8,128)} async-done(((f32[1024,4096]{1,0:T(8,128)}), f32[32,4096]{1,0:T(8,128)}) %reduce-scatter.9.cloned.1.call-update) | async-done | bytes 524304 | tf_op jit(solution)/shard_map/reduce_scatter | solution.py:317
  903.8 187.5 %reduce-scatter.11.cloned.1.call-done = f32[128,1024]{1,0:T(8,128)} async-done(((f32[4096,1024]{1,0:T(8,128)}), f32[128,1024]{1,0:T(8,128)}) %reduce-scatter.11.cloned.1.call-update) | async-done | bytes 524304 | tf_op jit(solution)/shard_map/reduce_scatter | solution.py:318
  (258 shorter events, 140.7 us)
Async XLA Ops:
  7.2 96.9 %all-gather.6.cloned.1.call-start = ((), (), s32[]{:S(2)}) async-start(), calls=%async_computation.4 | async-start | bytes 6488064 | tf_op jit(solution)/shard_map/all_gather | solution.py:262
  7.9 169.9 %all-gather.8.cloned.1.call-start = ((), (), s32[]{:S(2)}) async-start(), calls=%async_computation.5 | async-start | bytes 2162688 | tf_op jit(solution)/shard_map/all_gather | solution.py:263
  8.7 211.8 %all-gather.10.cloned.1.call-start = ((), (), s32[]{:S(2)}) async-start(), calls=%async_computation.6 | async-start | bytes 8650752 | tf_op jit(solution)/shard_map/all_gather | solution.py:264
  9.4 289.8 %all-gather.12.cloned.1.call-start = ((), (), s32[]{:S(2)}) async-start(), calls=%async_computation.7 | async-start | bytes 8650752 | tf_op jit(solution)/shard_map/all_gather | solution.py:265
  10.0 622.5 %reduce-scatter.7.cloned.1.call-start = ((), (), s32[]{:S(2)}) async-start(), calls=%async_computation.8 | async-start | bytes 4325376 | tf_op jit(solution)/shard_map/reduce_scatter | solution.py:316
  60.3 249.3 %copy-start.38 = (f32[1024]{0:T(1024)}, f32[1024]{0:T(1024)S(1)}, u32[]{:S(2)}) copy-start(f32[1024]{0:T(1024)S(1)} %convert_element_type.190) | copy-start | bytes 12292
  115.6 17.6 %copy-start.5 = (bf16[512,3072]{0,1:T(8,128)(2,1)}, bf16[512,3072]{0,1:T(8,128)(2,1)S(1)}, u32[]{:S(2)}) copy-start(bf16[512,3072]{0,1:T(8,128)(2,1)S(1)} %copy.76) | copy-start | bytes 9437188
  133.2 8.7 copy-start.25
  152.9 16.2 %copy-start.2 = (bf16[512,3072]{0,1:T(8,128)(2,1)}, bf16[512,3072]{0,1:T(8,128)(2,1)S(1)}, u32[]{:S(2)}) copy-start(bf16[512,3072]{0,1:T(8,128)(2,1)S(1)} %copy.78) | copy-start | bytes 9437188
  181.5 184.0 %copy-start.51 = (f32[512]{0:T(512)}, f32[512]{0:T(512)S(1)}, u32[]{:S(2)}) copy-start(f32[512]{0:T(512)S(1)} %broadcast_multiply_fusion.11) | copy-start | bytes 6148
  181.9 183.7 %copy-start.59 = (f32[512]{0:T(512)}, f32[512]{0:T(512)S(1)}, u32[]{:S(2)}) copy-start(f32[512]{0:T(512)S(1)} %add_rsqrt_fusion.3) | copy-start | bytes 6148
  183.3 231.8 %copy-start = (f32[512,1024]{1,0:T(8,128)}, f32[512,1024]{1,0:T(8,128)S(1)}, u32[]{:S(2)}) copy-start(f32[512,1024]{1,0:T(8,128)S(1)} %get-tuple-element.152) | copy-start | bytes 6291460
  220.5 10.5 copy-start.17
  220.5 10.5 copy-start.61
  230.9 68.3 %copy-start.58 = (f32[1024]{0:T(1024)S(1)}, f32[1024]{0:T(1024)}, u32[]{:S(2)}) copy-start(f32[1024]{0:T(1024)} %convert_element_type.194) | copy-start | bytes 12292
  299.2 10.4 copy-start.11
  299.3 10.4 copy-start.62
  321.5 44.1 %copy-start.21 = (f32[512,1024]{1,0:T(8,128)}, f32[512,1024]{1,0:T(8,128)S(1)}, u32[]{:S(2)}) copy-start(f32[512,1024]{1,0:T(8,128)S(1)} %get-tuple-element.121) | copy-start | bytes 6291460
  321.5 16.9 %copy-start.18 = (f32[512,1024]{1,0:T(8,128)S(1)}, f32[512,1024]{1,0:T(8,128)}, u32[]{:S(2)}) copy-start(f32[512,1024]{1,0:T(8,128)} %copy-done.16) | copy-start | bytes 6291460
  321.5 16.9 %copy-start.35 = (f32[512,1024]{1,0:T(8,128)S(1)}, f32[512,1024]{1,0:T(8,128)}, u32[]{:S(2)}) copy-start(f32[512,1024]{1,0:T(8,128)} %get-tuple-element.136) | copy-start | bytes 6291460
  365.6 12.7 %copy-start.24 = (bf16[16,64,512]{2,1,0:T(8,128)(2,1)S(1)}, bf16[16,64,512]{2,1,0:T(8,128)(2,1)}, u32[]{:S(2)}) copy-start(bf16[16,64,512]{2,1,0:T(8,128)(2,1)} %fusion.41) | copy-start | bytes 3145732
  396.7 12.3 %copy-start.6 = (bf16[512,3072]{0,1:T(8,128)(2,1)S(1)}, bf16[512,3072]{0,1:T(8,128)(2,1)}, u32[]{:S(2)}) copy-start(bf16[512,3072]{0,1:T(8,128)(2,1)} %copy-done.5) | copy-start | bytes 9437188
  421.5 297.4 %reduce-scatter.13.cloned.1.call-start = ((), (), s32[]{:S(2)}) async-start(), calls=%async_computation.11 | async-start | bytes 12976128
  452.1 29.6 %slice-start = ((s8[16777216]{0:T(1024)(128)(4,1)}), s8[4194304]{0:T(1024)(128)(4,1)S(1)}, s32[]{:S(2)}) async-start(s8[16777216]{0:T(1024)(128)(4,1)} %bitcast.123), calls=%async_computation.12 | async-start | bytes 8388608
  452.1 29.6 %slice-start.1 = ((s8[16777216]{0:T(1024)(128)(4,1)}), s8[4194304]{0:T(1024)(128)(4,1)S(1)}, s32[]{:S(2)}) async-start(s8[16777216]{0:T(1024)(128)(4,1)} %bitcast.123), calls=%async_computation.13 | async-start | bytes 8388608
  452.1 29.6 %slice-start.2 = ((s8[16777216]{0:T(1024)(128)(4,1)}), s8[4194304]{0:T(1024)(128)(4,1)S(1)}, s32[]{:S(2)}) async-start(s8[16777216]{0:T(1024)(128)(4,1)} %bitcast.123), calls=%async_computation.14 | async-start | bytes 8388608
  512.2 391.6 %reduce-scatter.9.cloned.1.call-start = ((), (), s32[]{:S(2)}) async-start(), calls=%async_computation.9 | async-start | bytes 17301504 | tf_op jit(solution)/shard_map/reduce_scatter | solution.py:317
  512.8 13.4 %copy-start.1 = (f32[512,1024]{1,0:T(8,128)S(1)}, f32[512,1024]{1,0:T(8,128)}, u32[]{:S(2)}) copy-start(f32[512,1024]{1,0:T(8,128)} %copy-done) | copy-start | bytes 6291460
  512.8 13.4 %copy-start.28 = (bf16[512,4096]{1,0:T(8,128)(2,1)S(1)}, bf16[512,4096]{1,0:T(8,128)(2,1)}, u32[]{:S(2)}) copy-start(bf16[512,4096]{1,0:T(8,128)(2,1)} %get-tuple-element.167) | copy-start | bytes 12582916
  538.4 552.9 %reduce-scatter.11.cloned.1.call-start = ((), (), s32[]{:S(2)}) async-start(), calls=%async_computation.10 | async-start | bytes 17301504 | tf_op jit(solution)/shard_map/reduce_scatter | solution.py:318
  538.4 13.3 %copy-start.12 = (bf16[512,4096]{1,0:T(8,128)(2,1)S(1)}, bf16[512,4096]{1,0:T(8,128)(2,1)}, u32[]{:S(2)}) copy-start(bf16[512,4096]{1,0:T(8,128)(2,1)} %get-tuple-element.137) | copy-start | bytes 12582916
  538.4 13.3 %copy-start.22 = (f32[512,1024]{1,0:T(8,128)S(1)}, f32[512,1024]{1,0:T(8,128)}, u32[]{:S(2)}) copy-start(f32[512,1024]{1,0:T(8,128)} %copy-done.21) | copy-start | bytes 6291460
  (44 other events, 132.9 us)
Sparse Core Ops, SparseCore 0:
  10.9 72.2 all-gather.5
  86.1 55.1 all-gather.7
  144.1 76.2 all-gather.9
  223.2 76.0 all-gather.11
  421.6 139.4 reduce-scatter.6
  567.6 151.3 reduce-scatter.12
  721.9 181.8 reduce-scatter.8
  906.7 184.4 reduce-scatter.10
where the time goes:
time: 1100 us
  waiting for transfers between devices  517 us (47%)
  matrix products  324 us (29%)
  blocking collectives  123 us (11%)
  other arithmetic  72.1 us (7%)
  local copies, waits for them, and re-layouts  45.4 us (4%)
  between operations  15.3 us (1%)
    reduce_scatter x1, waiting for transfers between devices, body(): lax.psum_scatter(sum_down, 'dp', scatter_dimension=0, tiled=True)  187 us
    reduce_scatter x1, waiting for transfers between devices, body(): lax.psum_scatter(sum_up, 'dp', scatter_dimension=0, tiled=True)  185 us
    unnamed x9, waiting for transfers between devices  89.1 us
    unnamed x2, blocking collectives  82.5 us
    dot_general x2, matrix products, forward_block(): jnp.dot(hidden_low, whole_up, preferred_element_type=jnp.float32)  56.2 us
    all_gather x1, blocking collectives, body(): lax.all_gather(up_bias, 'dp', axis=0, tiled=True)  40.8 us
    all_gather x1, waiting for transfers between devices, body(): lax.all_gather(up_weight, 'dp', axis=0, tiled=True)  36.8 us
    unnamed x163, local copies, waits for them, and re-layouts  34.3 us
  transfers between devices with their start and end apart: 8, of which 5 were waited for; matrix products, arithmetic and copies ran while one was open for 28% of the time, Pallas kernels for 0%

commit v1 on v0

v1 whole, which is shorter than its diff:
```python
import functools
import math

import jax
import jax.numpy as jnp
from jax import lax
from jax.experimental import pallas as pl
from jax.experimental.pallas import tpu as pltpu
from jax.sharding import PartitionSpec as P

HEADS = 16
HEAD_SIZE = 64
LANES = 128
epsilon = 1e-05
VMEM_BYTES = 48 * 1024 * 1024
F32 = jnp.float32
BF16 = jnp.bfloat16


def dot(left, right, left_dim, right_dim):
    return lax.dot_general(
        left, right, (((left_dim,), (right_dim,)), ((), ())), preferred_element_type=F32
    )


def norm_rows(values, norm_gain, norm_shift):
    center = values - jnp.mean(values, axis=-1, keepdims=True)
    variance = jnp.mean(center * center, axis=-1, keepdims=True)
    inverse = lax.rsqrt(variance + epsilon)
    scaled = center * inverse
    return (scaled * norm_gain + norm_shift, scaled, inverse)


def norm_back(gradient, scaled, inverse, norm_gain):
    weighted = gradient * norm_gain
    mean_grad = jnp.mean(weighted, axis=-1, keepdims=True)
    mean_prod = jnp.mean(weighted * scaled, axis=-1, keepdims=True)
    result = inverse * (weighted - mean_grad - scaled * mean_prod)
    return (result, jnp.sum(gradient * scaled, axis=0), jnp.sum(gradient, axis=0))


def head_probs(query, key, allowed):
    scores = jnp.where(allowed, dot(query, key, 1, 1), -1e30)
    expo = jnp.exp(scores - jnp.max(scores, axis=-1, keepdims=True))
    return expo * (1.0 / jnp.sum(expo, axis=-1, keepdims=True))


def attend_kernel(column_ref, row_ref, query_ref, key_ref, value_ref, out_ref):
    allowed = column_ref[...] == row_ref[...]
    for start in range(0, LANES, HEAD_SIZE):
        part = slice(start, start + HEAD_SIZE)
        query = query_ref[:, part] * jnp.asarray(HEAD_SIZE**-0.5, BF16)
        probs = head_probs(query, key_ref[:, part], allowed)
        out_ref[:, part] = dot(probs.astype(BF16), value_ref[:, part], 1, 0).astype(BF16)


def attend_back_kernel(
    column_ref, row_ref, query_ref, key_ref, value_ref, grad_ref, dq_ref, dk_ref, dv_ref
):
    allowed = column_ref[...] == row_ref[...]
    factor = HEAD_SIZE**-0.5
    for start in range(0, LANES, HEAD_SIZE):
        part = slice(start, start + HEAD_SIZE)
        query = query_ref[:, part] * jnp.asarray(factor, BF16)
        key = key_ref[:, part]
        grad = grad_ref[:, part]
        probs = head_probs(query, key, allowed)
        dv_ref[:, part] = dot(probs.astype(BF16), grad, 0, 0).astype(BF16)
        grad_probs = dot(grad, value_ref[:, part], 1, 1)
        weighted = probs * grad_probs
        low = (weighted - probs * jnp.sum(weighted, axis=-1, keepdims=True)).astype(BF16)
        dq_ref[:, part] = (dot(low, key, 1, 0) * factor).astype(BF16)
        dk_ref[:, part] = dot(low, query, 0, 0).astype(BF16)


def attention_call(kernel, outs, labels, mixed, extra):
    micro_count, slot = labels.shape
    rows, width = mixed.shape
    width = width // 3
    groups = width // LANES

    def part(offset):
        return pl.BlockSpec((slot, LANES), lambda b, h: (b, offset + h))

    return pl.pallas_call(
        kernel,
        grid=(micro_count, groups),
        in_specs=[
            pl.BlockSpec((slot, 1), lambda b, h: (b, 0)),
            pl.BlockSpec((None, 1, slot), lambda b, h: (b, 0, 0)),
            part(0),
            part(groups),
            part(2 * groups),
        ]
        + [part(0)] * len(extra),
        out_specs=[part(0)] * outs,
        out_shape=[jax.ShapeDtypeStruct((rows, width), BF16)] * outs,
        compiler_params=pltpu.CompilerParams(vmem_limit_bytes=VMEM_BYTES),
        cost_estimate=pl.CostEstimate(
            flops=rows * slot * width * 4 * (1 + 2 * outs // 3 * 2),
            bytes_accessed=rows * width * 2 * (3 + outs + len(extra)),
            transcendentals=rows * slot * HEADS,
        ),
    )(labels.reshape(rows, 1), labels.reshape(micro_count, 1, slot), mixed, mixed, mixed, *extra)


def up_kernel(hidden_ref, weight_ref, bias_ref, activ_ref, slope_ref):
    pre_act = dot(hidden_ref[...], weight_ref[...], 1, 0) + bias_ref[...]
    cumulative = 0.5 + 0.5 * lax.erf(pre_act * math.sqrt(0.5))
    density = jnp.exp(-0.5 * pre_act * pre_act) * (1.0 / math.sqrt(2.0 * math.pi))
    activ_ref[...] = (pre_act * cumulative).astype(BF16)
    slope_ref[...] = (cumulative + pre_act * density).astype(BF16)


def up_call(hidden_low, weight, bias):
    rows, width = hidden_low.shape
    units = weight.shape[1]
    block = 512
    tall = rows // 2
    return pl.pallas_call(
        up_kernel,
        grid=(units // block, 2),
        in_specs=[
            pl.BlockSpec((tall, width), lambda i, j: (j, 0)),
            pl.BlockSpec((width, block), lambda i, j: (0, i)),
            pl.BlockSpec((1, block), lambda i, j: (0, i)),
        ],
        out_specs=[pl.BlockSpec((tall, block), lambda i, j: (j, i))] * 2,
        out_shape=[jax.ShapeDtypeStruct((rows, units), BF16)] * 2,
        compiler_params=pltpu.CompilerParams(vmem_limit_bytes=VMEM_BYTES),
        cost_estimate=pl.CostEstimate(
            flops=2 * rows * width * units,
            bytes_accessed=2 * (width * units + 2 * rows * units),
            transcendentals=2 * rows * units,
        ),
    )(hidden_low, weight, bias.reshape(1, units))


def halve(blocks, bits_left, bit, device, count, final):
    axis = bits_left.index(bit)
    mine = (device >> bit) & 1
    kept = lax.dynamic_index_in_dim(blocks, mine, axis, keepdims=False)
    sent = lax.dynamic_index_in_dim(blocks, 1 - mine, axis, keepdims=False)
    partners = [(i, i ^ (1 << bit)) for i in range(count)]
    arrived = lax.ppermute(sent, "dp", partners)
    total = kept.astype(F32) + arrived.astype(F32)
    left = [other for other in bits_left if other != bit]
    return (total if final else total.astype(blocks.dtype), left)


def scatter_sum(blocks, orders, device, count):
    levels = count.bit_length() - 1
    columns = blocks.shape[-1]
    tail = blocks.shape[1:]
    left = list(range(levels - 1, -1, -1))
    split = blocks.reshape((2,) * levels + tail)
    split, left = halve(split, left, 0, device, count, levels == 1)
    pieces = []
    width = columns // len(orders)
    for index, order in enumerate(orders):
        part = lax.slice_in_dim(split, index * width, (index + 1) * width, axis=split.ndim - 1)
        rest = left
        for step, bit in enumerate(order):
            part, rest = halve(part, rest, bit, device, count, step == len(order) - 1)
        pieces.append(part)
    return pieces[0] if len(pieces) == 1 else jnp.concatenate(pieces, axis=-1)


def body(
    count,
    inputs,
    seq_lengths,
    qkv_weight,
    out_weight,
    up_weight,
    down_weight,
    query_bias,
    value_bias,
    out_bias,
    up_bias,
    down_bias,
    first_gain,
    first_shift,
    second_gain,
    second_shift,
    grad_output,
):
    device = lax.axis_index("dp")
    levels = count.bit_length() - 1
    high = list(range(1, levels))
    order_one = high
    order_two = high[1:] + high[:1]
    rows, width = inputs.shape
    micro_count = seq_lengths.shape[0]
    slot = rows // micro_count

    small = (
        query_bias,
        value_bias,
        out_bias,
        up_bias,
        down_bias,
        first_gain,
        first_shift,
        second_gain,
        second_shift,
    )
    sizes = [vector.shape[0] for vector in small]
    packed = lax.all_gather(jnp.concatenate(small), "dp", axis=0, tiled=False)
    whole_qkv = lax.all_gather(qkv_weight, "dp", axis=0, tiled=True)
    whole_out = lax.all_gather(out_weight, "dp", axis=0, tiled=True)
    whole_up = lax.all_gather(up_weight, "dp", axis=0, tiled=True)
    whole_down = lax.all_gather(down_weight, "dp", axis=0, tiled=True)
    vectors = []
    start = 0
    for size in sizes:
        vectors.append(packed[:, start : start + size].reshape(-1).astype(F32))
        start += size
    (
        bias_query,
        bias_value,
        bias_out,
        bias_up,
        bias_down,
        gain_first,
        shift_first,
        gain_second,
        shift_second,
    ) = vectors

    seq_ends = jnp.cumsum(seq_lengths, axis=1)
    places = jnp.arange(slot, dtype=jnp.int32)
    labels = jnp.sum((places[None, :, None] >= seq_ends[:, None, :]).astype(jnp.int32), axis=2)

    bias_all = jnp.concatenate([bias_query, jnp.zeros_like(bias_query), bias_value])
    mixed_low = (dot(inputs, whole_qkv, 1, 0) + bias_all).astype(BF16)
    (attended_low,) = attention_call(attend_kernel, 1, labels, mixed_low, ())
    branch = dot(attended_low, whole_out, 1, 0) + bias_out
    hidden, scaled_first, inverse_first = norm_rows(
        inputs.astype(F32) + branch, gain_first, shift_first
    )
    hidden_low = hidden.astype(BF16)
    activ_low, slope_low = up_call(hidden_low, whole_up, bias_up)
    second = dot(activ_low, whole_down, 1, 0) + bias_down
    result, scaled_second, inverse_second = norm_rows(hidden + second, gain_second, shift_second)

    grad_second_in, grad_gain_two, grad_shift_two = norm_back(
        grad_output.astype(F32), scaled_second, inverse_second, gain_second
    )
    grad_branch_two = grad_second_in.astype(BF16)
    grad_down_bias = jnp.sum(grad_branch_two.astype(F32), axis=0)
    grad_down = dot(activ_low, grad_branch_two, 0, 0).astype(BF16)
    grad_down, grad_branch_two = lax.optimization_barrier((grad_down, grad_branch_two))
    sum_down = scatter_sum(
        grad_down.reshape(count, -1, width), (order_one, order_two), device, count
    )

    grad_pre = dot(grad_branch_two, whole_down, 1, 1) * slope_low.astype(F32)
    grad_pre_low = grad_pre.astype(BF16)
    grad_up_bias = jnp.sum(grad_pre_low.astype(F32), axis=0)
    grad_up = dot(hidden_low, grad_pre_low, 0, 0).astype(BF16)
    grad_up, grad_pre_low = lax.optimization_barrier((grad_up, grad_pre_low))
    sum_up = scatter_sum(
        grad_up.reshape(count, -1, grad_up.shape[1]), (order_one, order_two), device, count
    )

    grad_hidden = grad_second_in + dot(grad_pre_low, whole_up, 1, 1)
    grad_first_in, grad_gain_one, grad_shift_one = norm_back(
        grad_hidden, scaled_first, inverse_first, gain_first
    )
    grad_branch_one = grad_first_in.astype(BF16)
    grad_out_bias = jnp.sum(grad_branch_one.astype(F32), axis=0)
    grad_out = dot(attended_low, grad_branch_one, 0, 0).astype(BF16)
    grad_out, grad_branch_one = lax.optimization_barrier((grad_out, grad_branch_one))
    sum_out = scatter_sum(grad_out.reshape(count, -1, width), (order_two,), device, count)

    grad_attended = dot(grad_branch_one, whole_out, 1, 1).astype(BF16)
    grads = attention_call(attend_back_kernel, 3, labels, mixed_low, (grad_attended,))
    grad_mixed = jnp.concatenate(grads, axis=1)
    grad_query_bias = jnp.sum(grads[0].astype(F32), axis=0)
    grad_value_bias = jnp.sum(grads[2].astype(F32), axis=0)
    grad_qkv = dot(inputs, grad_mixed, 0, 0).astype(BF16)
    grad_qkv, grad_mixed = lax.optimization_barrier((grad_qkv, grad_mixed))
    sum_qkv = scatter_sum(
        grad_qkv.reshape(count, -1, 3 * width), (order_one, order_two), device, count
    )
    grad_small = jnp.concatenate(
        [
            vector.reshape(count, -1)
            for vector in (
                grad_query_bias,
                grad_value_bias,
                grad_out_bias,
                grad_up_bias,
                grad_down_bias,
                grad_gain_one,
                grad_shift_one,
                grad_gain_two,
                grad_shift_two,
            )
        ],
        axis=1,
    )
    sum_small = scatter_sum(grad_small[:, None, :], (order_one,), device, count)[0]
    grad_tokens = grad_first_in + dot(grad_mixed, whole_qkv, 1, 1)

    shares = []
    start = 0
    for size in sizes:
        shares.append(sum_small[start : start + size])
        start += size
    return (
        result.astype(BF16),
        grad_tokens.astype(BF16),
        sum_qkv,
        sum_out,
        sum_up,
        sum_down,
        *shares,
    )


def solution(mesh):
    matrix, vector = P("dp", None), P("dp")
    return jax.shard_map(
        functools.partial(body, mesh.shape["dp"]),
        mesh=mesh,
        in_specs=(matrix,) * 6 + (vector,) * 9 + (matrix,),
        out_specs=(matrix,) * 6 + (vector,) * 9,
        check_vma=False,
    )
```

time: 1100 us -> 678 us (0.62)
  waiting for transfers between devices: 517 us -> 256 us
  matrix products: 324 us -> 124 us
  Pallas kernels: 0 us -> 107 us
  blocking collectives: 123 us -> 43.4 us
  other arithmetic: 72.1 us -> 35 us
  starting transfers between devices: 0.32 us -> 34 us
    reduce_scatter x3 -> x0, waiting for transfers between devices: 372 us -> none  [the longest x1 187 us: body(): lax.psum_scatter(sum_down, 'dp', scatter_dimension=0, tiled=True)]
    dot_general x36 -> x11, matrix products: 324 us -> 124 us  [dot(): lax.dot_general(left, right, (((left_dim,), (right_dim,)), ((), ())), pre...]
    pallas_call x0 -> x3, Pallas kernels: none -> 107 us  [the longest x2 83.7 us: attention_call(): pl.pallas_call(kernel, grid=(micro_count, groups), in_specs=[pl.BlockSpec...]
    ppermute x0 -> x37, waiting for transfers between devices: none -> 101 us  [halve(): arrived = lax.ppermute(sent, 'dp', partners)]
    all_gather x4, waiting for transfers between devices: 56.1 us -> 153 us  [the longest x1 70.5 us: body(): whole_up = lax.all_gather(up_weight, 'dp', axis=0, tiled=True)]
    unnamed x9 -> x4, waiting for transfers between devices: 89.1 us -> 2.58 us
    unnamed x2 -> x0, blocking collectives: 82.5 us -> none
    ppermute x0 -> x37, starting transfers between devices: none -> 33.9 us  [halve(): arrived = lax.ppermute(sent, 'dp', partners)]
  transfers between devices with their start and end apart: 8 -> 41, of which waited for: 5 -> 23; matrix products, arithmetic and copies ran while one was open for 28% -> 16% of each run, Pallas kernels for 0% -> 10%
where the time goes in v1:
time: 678 us; the launch traced here: 668 us
  waiting for transfers between devices  256 us (38%)
  matrix products  124 us (18%)
  Pallas kernels  107 us (16%)
  local copies, waits for them, and re-layouts  53.4 us (8%)
  blocking collectives  43.4 us (6%)
  other arithmetic  35 us (5%)
  starting transfers between devices  34 us (5%)
  between operations  15.1 us (2%)
    dot_general x11, matrix products, dot(): lax.dot_general(left, right, (((left_dim,), (right_dim,)), ((), ())), pre...  124 us
    ppermute x37, waiting for transfers between devices, halve(): arrived = lax.ppermute(sent, 'dp', partners)  101 us
    pallas_call x2, Pallas kernels, attention_call(): pl.pallas_call(kernel, grid=(micro_count, groups), in_specs=[pl.BlockSpec...  83.7 us
    all_gather x1, waiting for transfers between devices, body(): whole_up = lax.all_gather(up_weight, 'dp', axis=0, tiled=True)  70.5 us
    all_gather x1, waiting for transfers between devices, body(): whole_down = lax.all_gather(down_weight, 'dp', axis=0, tiled=True)  54 us
    all_gather x1, blocking collectives, body(): packed = lax.all_gather(jnp.concatenate(small), 'dp', axis=0, tiled=False)  43.4 us
    ppermute x37, starting transfers between devices, halve(): arrived = lax.ppermute(sent, 'dp', partners)  33.9 us
    pallas_call x1, Pallas kernels, up_call(): pl.pallas_call(up_kernel, grid=(units // block, 2), in_specs=[pl.BlockSpe...  23.2 us
  transfers between devices with their start and end apart: 41, of which 23 were waited for; matrix products, arithmetic and copies ran while one was open for 16% of the time, Pallas kernels for 10%

profile of v1, /device:TPU:0, one launch (start us, length us, event | category | flops | bytes accessed | tf_op | source)
XLA Modules:
  0.0 667.6 jit_solution(7114624769510785299)
XLA Ops:
  10.0 6.1 concatenate.40
  16.1 43.4 %all-gather.1 = bf16[32,1,384]{2,1,0:T(2,128)(2,1)S(1)} all-gather(bf16[1,1,384]{2,1,0:T(2,128)(2,1)S(1)} %reshape.294), channel_id=2, replica_groups=mesh['dp'=32] {'dp'}, dimensions={0}, use_global_device_ids=true | all-gather | bytes 25344 | tf_op jit(solution)/shard_map/all_gather | solution.py:209
  61.5 21.7 %all-gather.7.cloned.1.call-done = bf16[1024,3072]{1,0:T(8,128)(2,1)} async-done(((bf16[32,3072]{1,0:T(8,128)(2,1)}), bf16[1024,3072]{1,0:T(8,128)(2,1)}) %all-gather.7.cloned.1.call-update) | async-done | bytes 6291472 | tf_op jit(solution)/shard_map/all_gather | solution.py:210
  83.2 11.0 %add_convert_fusion.query_ref.key_ref.value_ref = bf16[1024,3072]{1,0:T(8,128)(2,1)} fusion(f32[3072]{0:T(1024)S(1)} %pad_maximum_fusion.3, bf16[1024,1024]{1,0:T(8,128)(2,1)} %param.16, bf16[1024,3072]{1,0:T(8,128)(2,1)} %all-gather.7.cloned.1.call-done), kind=kOutput, calls=%fused_computation.2 | convolution fusion | flops 6448742400 | bytes 14692352 | tf_op jit(solution)/shard_map/dot_general | solution.py:21
  94.2 40.4 %shard_map.271 = bf16[1024,1024]{1,0:T(8,128)(2,1)S(1)} custom-call(s32[1024,1]{1,0:T(8,128)S(1)} %bitcast.255, s32[2,1,512]{2,1,0:T(1,128)S(1)} %reshape.251.row_ref, bf16[1024,3072]{1,0:T(8,128)(2,1)} %add_convert_fusion.query_ref.key_ref.value_ref, bf16[1024,3072]{1,0:T(8,128)(2,1)} %add_convert_fusion.query_ref.key_ref.value_ref, ...), custom_call_target="tpu_custom_call" | custom-call | flops 2147483648 | bytes 8388608 | tf_op jit(solution)/shard_map/pallas_call | solution.py:85
  134.6 6.4 all-gather.9.cloned.1.call-done
  141.0 4.7 fusion.50
  149.7 70.5 %all-gather.11.cloned.1.call-done.weight_ref = bf16[1024,4096]{1,0:T(8,128)(2,1)} async-done(((bf16[32,4096]{1,0:T(8,128)(2,1)}), bf16[1024,4096]{1,0:T(8,128)(2,1)}) %all-gather.11.cloned.1.call-update) | async-done | bytes 8388624 | tf_op jit(solution)/shard_map/all_gather | solution.py:212
  221.8 23.2 %shard_map.272 = (bf16[1024,4096]{1,0:T(8,128)(2,1)}, bf16[1024,4096]{1,0:T(8,128)(2,1)}) custom-call(bf16[1024,1024]{1,0:T(8,128)(2,1)S(1)} %copy-done, bf16[1024,4096]{1,0:T(8,128)(2,1)} %all-gather.11.cloned.1.call-done.weight_ref, f32[1,4096]{1,0:T(1,128)S(1)} %bitcast.257), custom_call_target="tpu_custom_call" | custom-call | flops 8589934592 | bytes 25165824 | tf_op jit(solution)/shard_map/pallas_call | solution.py:120
  245.0 54.0 %all-gather.13.cloned.1.call-done = bf16[4096,1024]{1,0:T(8,128)(2,1)} async-done(((bf16[128,1024]{1,0:T(8,128)(2,1)}), bf16[4096,1024]{1,0:T(8,128)(2,1)}) %all-gather.13.cloned.1.call-update) | async-done | bytes 8388624 | tf_op jit(solution)/shard_map/all_gather | solution.py:213
  299.0 15.0 %fusion.51 = (f32[1024]{0:T(1024)S(1)}, f32[1024,1024]{1,0:T(8,128)S(1)}) fusion(f32[1024]{0:T(1024)S(1)} %reshape.258, bf16[1024,4096]{1,0:T(8,128)(2,1)} %get-tuple-element.28, bf16[4096,1024]{1,0:T(8,128)(2,1)} %all-gather.13.cloned.1.call-done, f32[1024]{0:T(1024)S(1)} %reshape.256, f32[1024]{0:T(1024)S(1)} %reshape.255, ...), kind=kOutput, calls=%fused_computation.201 | convolution fusion | flops 8597273600 | bytes 25190400 | tf_op jit(solution)/shard_map/dot_general | solution.py:21
  322.4 11.3 %convolution_convert_fusion.1 = bf16[4096,1024]{1,0:T(8,128)(2,1)} fusion(bf16[1024,4096]{1,0:T(8,128)(2,1)S(1)} %bitcast.272, bf16[1024,1024]{1,0:T(8,128)(2,1)S(1)} %get-tuple-element.29), kind=kOutput, calls=%fused_computation.8 | convolution fusion | flops 8594128896 | bytes 18874368 | tf_op jit(solution)/shard_map/dot_general | solution.py:21
  333.7 16.0 %convert_reduce_fusion = (f32[4096]{0:T(1024)S(1)}, bf16[1024,4096]{1,0:T(8,128)(2,1)}) fusion(bf16[1024,4096]{1,0:T(8,128)(2,1)} %get-tuple-element.30, bf16[1024,1024]{1,0:T(8,128)(2,1)} %copy-done.10, bf16[4096,1024]{1,0:T(8,128)(2,1)} %all-gather.13.cloned.1.call-done), kind=kOutput, calls=%fused_computation | convolution fusion | flops 8610902016 | bytes 27279360 | tf_op jit(solution)/shard_map/dot_general | solution.py:21
  349.7 15.2 %convolution_convert_fusion = bf16[1024,4096]{1,0:T(8,128)(2,1)} fusion(bf16[1024,1024]{1,0:T(8,128)(2,1)} %fusion.10.hidden_ref, bf16[1024,4096]{1,0:T(8,128)(2,1)} %get-tuple-element.31), kind=kOutput, calls=%fused_computation.7 | convolution fusion | flops 8594128896 | bytes 18874368 | tf_op jit(solution)/shard_map/dot_general | solution.py:21
  364.9 19.5 %multiply_reduce_fusion = (f32[1024]{0:T(1024)S(1)}, f32[1024]{0:T(1024)S(1)}, f32[1024]{0:T(1024)S(1)}, f32[1024]{0:T(1024)S(1)}, f32[1024,1024]{1,0:T(8,128)}) fusion(f32[1024,1024]{1,0:T(8,128)} %copy-done.2, f32[1024]{0:T(1024)S(1)} %add_rsqrt_fusion.1, f32[1024]{0:T(1024)S(1)} %broadcast_multiply_fusion.5, f32[1024]{0:T(1024)S(1)} %reshape.255, ...), kind=kOutput, calls=%fused_computation.26 | convolution fusion | flops 8608804864 | bytes 31506432 | tf_op jit(solution)/shard_map/dot_general | solution.py:21
  384.5 5.7 convert_reduce_fusion.3
  397.7 43.4 %shard_map.273 = (bf16[1024,1024]{1,0:T(8,128)(2,1)S(1)}, bf16[1024,1024]{1,0:T(8,128)(2,1)S(1)}, bf16[1024,1024]{1,0:T(8,128)(2,1)}) custom-call(s32[1024,1]{1,0:T(8,128)S(1)} %bitcast.256, s32[2,1,512]{2,1,0:T(1,128)S(1)} %reshape.251.row_ref, bf16[1024,3072]{1,0:T(8,128)(2,1)} %add_convert_fusion.query_ref.key_ref.value_ref, ...), custom_call_target="tpu_custom_call" | custom-call | flops 10737418240 | bytes 14680064 | tf_op jit(solution)/shard_map/pallas_call | solution.py:85
  446.4 7.0 %constant_dynamic-slice_fusion.9 = (bf16[2,2,2,2,1,128,1024]{6,5,4,3,2,1,0:T(8,128)(2,1)}, bf16[2,2,2,2,1,128,1024]{6,5,4,3,2,1,0:T(8,128)(2,1)S(1)}) fusion(bf16[2,2,2,2,2,128,1024]{6,5,4,3,2,1,0:T(8,128)(2,1)} %bitcast.263, s32[]{:T(128)S(6)} %select_n.128, s32[]{:T(128)S(6)} %select_n.129), kind=kLoop, calls=%fused_computation.145 | loop fusion | bytes 16777224 | tf_op jit(solution)/shard_map/jit(dynamic_index_in_dim)/dynamic_slice | solution.py:142
  456.3 6.3 constant_dynamic-slice_fusion.11
  474.6 11.7 %convert_bitcast_fusion = bf16[1024,3072]{0,1:T(8,128)(2,1)} fusion(bf16[1024,3072]{1,0:T(8,128)(2,1)} %constant_dynamic-update-slice_fusion, bf16[1024,1024]{1,0:T(8,128)(2,1)S(1)} %copy-done.11), kind=kOutput, calls=%fused_computation.11 | convolution fusion | flops 6445596672 | bytes 14680064 | tf_op jit(solution)/shard_map/dot_general | solution.py:21
  486.3 8.6 %copy.87 = bf16[1024,3072]{1,0:T(8,128)(2,1)} copy(bf16[1024,3072]{0,1:T(8,128)(2,1)} %convert_bitcast_fusion) | data formatting | bytes 12582912 | tf_op jit(solution)/shard_map/optimization_barrier | solution.py:283
  502.9 12.0 %add_convert_fusion.1 = bf16[1024,1024]{1,0:T(8,128)(2,1)} fusion(f32[1024,1024]{1,0:T(8,128)S(1)} %copy-done.8, bf16[1024,3072]{1,0:T(8,128)(2,1)} %constant_dynamic-update-slice_fusion, bf16[1024,3072]{1,0:T(8,128)(2,1)} %all-gather.7.cloned.1.call-done), kind=kOutput, calls=%fused_computation.31 | convolution fusion | flops 6444548096 | bytes 18874368 | tf_op jit(solution)/shard_map/dot_general | solution.py:21
  518.8 4.7 collective-permute-done.11
  533.1 13.5 %collective-permute-done.13 = bf16[32,1024]{1,0:T(8,128)(2,1)S(1)} collective-permute-done((bf16[32,1024]{1,0:T(8,128)(2,1)S(1)}, bf16[32,1024]{1,0:T(8,128)(2,1)S(1)}, u32[]{:S(2)}, u32[]{:S(2)}) %collective-permute-start.13) | collective-permute-done | bytes 65568 | tf_op jit(solution)/shard_map/ppermute | solution.py:145
  550.3 4.3 fusion
  566.5 4.6 collective-permute-done.3
  573.2 7.5 %collective-permute-done.7 = bf16[2,32,1536]{2,1,0:T(8,128)(2,1)S(1)} collective-permute-done((bf16[2,32,1536]{2,1,0:T(8,128)(2,1)S(1)}, bf16[2,32,1536]{2,1,0:T(8,128)(2,1)S(1)}, u32[]{:S(2)}, u32[]{:S(2)}) %collective-permute-start.7) | collective-permute-done | bytes 196640 | tf_op jit(solution)/shard_map/ppermute | solution.py:145
  580.8 5.4 collective-permute-done.4
  588.0 12.4 %collective-permute-done.8 = bf16[32,1536]{1,0:T(8,128)(2,1)S(1)} collective-permute-done((bf16[32,1536]{1,0:T(8,128)(2,1)S(1)}, bf16[32,1536]{1,0:T(8,128)(2,1)S(1)}, u32[]{:S(2)}, u32[]{:S(2)}) %collective-permute-start.8) | collective-permute-done | bytes 98336 | tf_op jit(solution)/shard_map/ppermute | solution.py:145
  607.2 9.6 %collective-permute-done.25 = bf16[2,2,128,512]{3,2,0,1:T(8,128)(2,1)S(1)} collective-permute-done((bf16[2,2,128,512]{3,2,0,1:T(8,128)(2,1)S(1)}, bf16[2,2,128,512]{3,2,0,1:T(8,128)(2,1)S(1)}, u32[]{:S(2)}, u32[]{:S(2)}) %collective-permute-start.25) | collective-permute-done | bytes 524320 | tf_op jit(solution)/shard_map/ppermute | solution.py:145
  624.8 14.1 %collective-permute-done.20 = bf16[2,2,32,2048]{3,2,1,0:T(8,128)(2,1)S(1)} collective-permute-done((bf16[2,2,32,2048]{3,2,1,0:T(8,128)(2,1)S(1)}, bf16[2,2,32,2048]{3,2,1,0:T(8,128)(2,1)S(1)}, u32[]{:S(2)}, u32[]{:S(2)}) %collective-permute-start.20) | collective-permute-done | bytes 524320 | tf_op jit(solution)/shard_map/ppermute | solution.py:145
  648.3 6.3 collective-permute-done.21
  (239 shorter events, 116.8 us)
Async XLA Ops:
  7.2 76.0 %all-gather.7.cloned.1.call-start = ((), (), s32[]{:S(2)}) async-start(), calls=%async_computation | async-start | bytes 6488064 | tf_op jit(solution)/shard_map/all_gather | solution.py:210
  7.9 133.1 %all-gather.9.cloned.1.call-start = ((), (), s32[]{:S(2)}) async-start(), calls=%async_computation.1 | async-start | bytes 2162688 | tf_op jit(solution)/shard_map/all_gather | solution.py:211
  8.7 211.5 %all-gather.11.cloned.1.call-start = ((), (), s32[]{:S(2)}) async-start(), calls=%async_computation.2 | async-start | bytes 8650752 | tf_op jit(solution)/shard_map/all_gather | solution.py:212
  9.4 289.6 %all-gather.13.cloned.1.call-start = ((), (), s32[]{:S(2)}) async-start(), calls=%async_computation.3 | async-start | bytes 8650752 | tf_op jit(solution)/shard_map/all_gather | solution.py:213
  446.1 23.1 %collective-permute-start.32 = (f32[2,2,2,2,1,384]{5,4,3,2,1,0:T(1,128)S(1)}, f32[2,2,2,2,1,384]{5,4,3,2,1,0:T(1,128)S(1)}, u32[]{:S(2)}, u32[]{:S(2)}) collective-permute-start(f32[2,2,2,2,1,384]{5,4,3,2,1,0:T(1,128)S(1)} %dynamic-slice_bitcast_fusion.28), channel_id=1, source_target_pairs={{0,1},{1,0},{2,3},{3,2},{4,5},{5,4},{6,7},{7,6},{8,9},{9,8},{10,11... | collective-permute-start | bytes 73736 | tf_op jit(solution)/shard_map/ppermute | solution.py:145
  456.0 94.3 %collective-permute-start.23 = (bf16[2,2,2,2,128,1024]{5,4,3,0,1,2:T(8,128)(2,1)}, bf16[2,2,2,2,128,1024]{5,4,3,0,1,2:T(8,128)(2,1)}, u32[]{:S(2)}, u32[]{:S(2)}) collective-permute-start(bf16[2,2,2,2,128,1024]{5,4,3,0,1,2:T(8,128)(2,1)} %bitcast.250), channel_id=1, source_target_pairs={{0,1},{1,0},{2,3},{3,2},{4,5},{5,4},{6,7},{7,6},{8,9},{9,8},{10,11... | collective-permute-start | bytes 12582920 | tf_op jit(solution)/shard_map/ppermute | solution.py:145
  464.8 92.9 %collective-permute-start.14 = (bf16[2,2,2,2,32,4096]{5,4,3,0,1,2:T(8,128)(2,1)}, bf16[2,2,2,2,32,4096]{5,4,3,0,1,2:T(8,128)(2,1)}, u32[]{:S(2)}, u32[]{:S(2)}) collective-permute-start(bf16[2,2,2,2,32,4096]{5,4,3,0,1,2:T(8,128)(2,1)} %bitcast.251), channel_id=1, source_target_pairs={{0,1},{1,0},{2,3},{3,2},{4,5},{5,4},{6,7},{7,6},{8,9},{9,8},{10,11... | collective-permute-start | bytes 12582920 | tf_op jit(solution)/shard_map/ppermute | solution.py:145
  467.3 33.3 %collective-permute-start.9 = (bf16[2,2,2,2,32,1024]{5,4,3,0,1,2:T(8,128)(2,1)}, bf16[2,2,2,2,32,1024]{5,4,3,0,1,2:T(8,128)(2,1)}, u32[]{:S(2)}, u32[]{:S(2)}) collective-permute-start(bf16[2,2,2,2,32,1024]{5,4,3,0,1,2:T(8,128)(2,1)} %bitcast.252), channel_id=1, source_target_pairs={{0,1},{1,0},{2,3},{3,2},{4,5},{5,4},{6,7},{7,6},{8,9},{9,8},{10,11... | collective-permute-start | bytes 3145736 | tf_op jit(solution)/shard_map/ppermute | solution.py:145
  473.0 21.9 %collective-permute-start.34 = (f32[2,2,1,384]{3,2,1,0:T(1,128)S(1)}, f32[2,2,1,384]{3,2,1,0:T(1,128)S(1)}, u32[]{:S(2)}, u32[]{:S(2)}) collective-permute-start(f32[2,2,1,384]{3,2,1,0:T(1,128)S(1)} %fusion.38), channel_id=1, source_target_pairs={{0,4},{1,5},{2,6},{3,7},{4,0},{5,1},{6,2},{7,3},{8,12},{9,13},{10,... | collective-permute-start | bytes 18440 | tf_op jit(solution)/shard_map/ppermute | solution.py:145
  498.9 27.0 %collective-permute-start = (bf16[2,2,2,2,32,3072]{5,4,3,2,1,0:T(8,128)(2,1)S(1)}, bf16[2,2,2,2,32,3072]{5,4,3,2,1,0:T(8,128)(2,1)S(1)}, u32[]{:S(2)}, u32[]{:S(2)}) collective-permute-start(bf16[2,2,2,2,32,3072]{5,4,3,2,1,0:T(8,128)(2,1)S(1)} %dynamic-slice_bitcast_fusion), channel_id=1, source_target_pairs={{0,1},{1,0},{2,3},{3,2},{4,5},{5,4},{6,7},{7,6},{8,9},{9,8},{10,11... | collective-permute-start | bytes 9437192 | tf_op jit(solution)/shard_map/ppermute | solution.py:145
  499.0 15.9 %collective-permute-start.36 = (f32[1,384]{1,0:T(1,128)S(1)}, f32[1,384]{1,0:T(1,128)S(1)}, u32[]{:S(2)}, u32[]{:S(2)}) collective-permute-start(f32[1,384]{1,0:T(1,128)S(1)} %fusion.44), channel_id=1, source_target_pairs={{0,16},{1,17},{2,18},{3,19},{4,20},{5,21},{6,22},{7,23},{8,24},{9,... | collective-permute-start | bytes 4616 | tf_op jit(solution)/shard_map/ppermute | solution.py:145
  502.3 13.5 %collective-permute-start.10 = (bf16[2,2,2,32,1024]{4,3,2,0,1:T(8,128)(2,1)S(1)}, bf16[2,2,2,32,1024]{4,3,2,0,1:T(8,128)(2,1)S(1)}, u32[]{:S(2)}, u32[]{:S(2)}) collective-permute-start(bf16[2,2,2,32,1024]{4,3,2,0,1:T(8,128)(2,1)S(1)} %dynamic-slice_bitcast_fusion.10), channel_id=1, source_target_pairs={{0,4},{1,5},{2,6},{3,7},{4,0},{5,1},{6,2},{7,3},{8,12},{9,13},{10,... | collective-permute-start | bytes 1572872 | tf_op jit(solution)/shard_map/ppermute | solution.py:145
  527.6 19.8 %collective-permute-start.1 = (bf16[2,2,2,32,1536]{4,3,0,1,2:T(8,128)(2,1)S(1)}, bf16[2,2,2,32,1536]{4,3,0,1,2:T(8,128)(2,1)S(1)}, u32[]{:S(2)}, u32[]{:S(2)}) collective-permute-start(bf16[2,2,2,32,1536]{4,3,0,1,2:T(8,128)(2,1)S(1)} %bitcast.265), channel_id=1, source_target_pairs={{0,2},{1,3},{2,0},{3,1},{4,6},{5,7},{6,4},{7,5},{8,10},{9,11},{10,... | collective-permute-start | bytes 2359304 | tf_op jit(solution)/shard_map/ppermute | solution.py:145
  531.0 15.7 %collective-permute-start.13 = (bf16[32,1024]{1,0:T(8,128)(2,1)S(1)}, bf16[32,1024]{1,0:T(8,128)(2,1)S(1)}, u32[]{:S(2)}, u32[]{:S(2)}) collective-permute-start(bf16[32,1024]{1,0:T(8,128)(2,1)S(1)} %dynamic-slice_bitcast_fusion.27), channel_id=1, source_target_pairs={{0,2},{1,3},{2,0},{3,1},{4,6},{5,7},{6,4},{7,5},{8,10},{9,11},{10,... | collective-permute-start | bytes 196616 | tf_op jit(solution)/shard_map/ppermute | solution.py:145
  532.1 17.9 %collective-permute-start.5 = (bf16[2,2,2,32,1536]{4,3,2,1,0:T(8,128)(2,1)S(1)}, bf16[2,2,2,32,1536]{4,3,2,1,0:T(8,128)(2,1)S(1)}, u32[]{:S(2)}, u32[]{:S(2)}) collective-permute-start(bf16[2,2,2,32,1536]{4,3,2,1,0:T(8,128)(2,1)S(1)} %dynamic-slice_bitcast_fusion.5), channel_id=1, source_target_pairs={{0,4},{1,5},{2,6},{3,7},{4,0},{5,1},{6,2},{7,3},{8,12},{9,13},{10,... | collective-permute-start | bytes 2359304 | tf_op jit(solution)/shard_map/ppermute | solution.py:145
  547.6 15.8 %collective-permute-start.2 = (bf16[2,2,32,1536]{3,2,0,1:T(8,128)(2,1)S(1)}, bf16[2,2,32,1536]{3,2,0,1:T(8,128)(2,1)S(1)}, u32[]{:S(2)}, u32[]{:S(2)}) collective-permute-start(bf16[2,2,32,1536]{3,2,0,1:T(8,128)(2,1)S(1)} %dynamic-slice_bitcast_fusion.12), channel_id=1, source_target_pairs={{0,4},{1,5},{2,6},{3,7},{4,0},{5,1},{6,2},{7,3},{8,12},{9,13},{10,... | collective-permute-start | bytes 1179656 | tf_op jit(solution)/shard_map/ppermute | solution.py:145
  550.2 14.0 %collective-permute-start.6 = (bf16[2,2,32,1536]{3,2,1,0:T(8,128)(2,1)S(1)}, bf16[2,2,32,1536]{3,2,1,0:T(8,128)(2,1)S(1)}, u32[]{:S(2)}, u32[]{:S(2)}) collective-permute-start(bf16[2,2,32,1536]{3,2,1,0:T(8,128)(2,1)S(1)} %dynamic-slice_bitcast_fusion.11), channel_id=1, source_target_pairs={{0,8},{1,9},{2,10},{3,11},{4,12},{5,13},{6,14},{7,15},{8,0},{9,1},... | collective-permute-start | bytes 1179656 | tf_op jit(solution)/shard_map/ppermute | solution.py:145
  555.3 45.9 %collective-permute-start.24 = (bf16[2,2,2,128,512]{4,3,0,1,2:T(8,128)(2,1)S(1)}, bf16[2,2,2,128,512]{4,3,0,1,2:T(8,128)(2,1)S(1)}, u32[]{:S(2)}, u32[]{:S(2)}) collective-permute-start(bf16[2,2,2,128,512]{4,3,0,1,2:T(8,128)(2,1)S(1)} %dynamic-slice_bitcast_fusion.2), channel_id=1, source_target_pairs={{0,2},{1,3},{2,0},{3,1},{4,6},{5,7},{6,4},{7,5},{8,10},{9,11},{10,... | collective-permute-start | bytes 3145736 | tf_op jit(solution)/shard_map/ppermute | solution.py:145
  556.9 46.0 %collective-permute-start.28 = (bf16[2,2,2,128,512]{4,3,2,0,1:T(8,128)(2,1)S(1)}, bf16[2,2,2,128,512]{4,3,2,0,1:T(8,128)(2,1)S(1)}, u32[]{:S(2)}, u32[]{:S(2)}) collective-permute-start(bf16[2,2,2,128,512]{4,3,2,0,1:T(8,128)(2,1)S(1)} %dynamic-slice_bitcast_fusion.1), channel_id=1, source_target_pairs={{0,4},{1,5},{2,6},{3,7},{4,0},{5,1},{6,2},{7,3},{8,12},{9,13},{10,... | collective-permute-start | bytes 3145736 | tf_op jit(solution)/shard_map/ppermute | solution.py:145
  562.0 43.1 %collective-permute-start.15 = (bf16[2,2,2,32,2048]{4,3,0,1,2:T(8,128)(2,1)S(1)}, bf16[2,2,2,32,2048]{4,3,0,1,2:T(8,128)(2,1)S(1)}, u32[]{:S(2)}, u32[]{:S(2)}) collective-permute-start(bf16[2,2,2,32,2048]{4,3,0,1,2:T(8,128)(2,1)S(1)} %dynamic-slice_bitcast_fusion.4), channel_id=1, source_target_pairs={{0,2},{1,3},{2,0},{3,1},{4,6},{5,7},{6,4},{7,5},{8,10},{9,11},{10,... | collective-permute-start | bytes 3145736 | tf_op jit(solution)/shard_map/ppermute | solution.py:145
  563.4 43.0 %collective-permute-start.19 = (bf16[2,2,2,32,2048]{4,3,2,0,1:T(8,128)(2,1)S(1)}, bf16[2,2,2,32,2048]{4,3,2,0,1:T(8,128)(2,1)S(1)}, u32[]{:S(2)}, u32[]{:S(2)}) collective-permute-start(bf16[2,2,2,32,2048]{4,3,2,0,1:T(8,128)(2,1)S(1)} %dynamic-slice_bitcast_fusion.3), channel_id=1, source_target_pairs={{0,4},{1,5},{2,6},{3,7},{4,0},{5,1},{6,2},{7,3},{8,12},{9,13},{10,... | collective-permute-start | bytes 3145736 | tf_op jit(solution)/shard_map/ppermute | solution.py:145
  586.3 14.1 %collective-permute-start.8 = (bf16[32,1536]{1,0:T(8,128)(2,1)S(1)}, bf16[32,1536]{1,0:T(8,128)(2,1)S(1)}, u32[]{:S(2)}, u32[]{:S(2)}) collective-permute-start(bf16[32,1536]{1,0:T(8,128)(2,1)S(1)} %dynamic-slice_bitcast_fusion.25), channel_id=1, source_target_pairs={{0,2},{1,3},{2,0},{3,1},{4,6},{5,7},{6,4},{7,5},{8,10},{9,11},{10,... | collective-permute-start | bytes 294920 | tf_op jit(solution)/shard_map/ppermute | solution.py:145
  601.6 15.3 %collective-permute-start.25 = (bf16[2,2,128,512]{3,2,0,1:T(8,128)(2,1)S(1)}, bf16[2,2,128,512]{3,2,0,1:T(8,128)(2,1)S(1)}, u32[]{:S(2)}, u32[]{:S(2)}) collective-permute-start(bf16[2,2,128,512]{3,2,0,1:T(8,128)(2,1)S(1)} %dynamic-slice_bitcast_fusion.7), channel_id=1, source_target_pairs={{0,4},{1,5},{2,6},{3,7},{4,0},{5,1},{6,2},{7,3},{8,12},{9,13},{10,... | collective-permute-start | bytes 1572872 | tf_op jit(solution)/shard_map/ppermute | solution.py:145
  603.4 17.7 %collective-permute-start.29 = (bf16[2,2,128,512]{3,2,1,0:T(8,128)(2,1)S(1)}, bf16[2,2,128,512]{3,2,1,0:T(8,128)(2,1)S(1)}, u32[]{:S(2)}, u32[]{:S(2)}) collective-permute-start(bf16[2,2,128,512]{3,2,1,0:T(8,128)(2,1)S(1)} %dynamic-slice_bitcast_fusion.6), channel_id=1, source_target_pairs={{0,8},{1,9},{2,10},{3,11},{4,12},{5,13},{6,14},{7,15},{8,0},{9,1},... | collective-permute-start | bytes 1572872 | tf_op jit(solution)/shard_map/ppermute | solution.py:145
  605.6 19.0 %collective-permute-start.16 = (bf16[2,2,32,2048]{3,2,0,1:T(8,128)(2,1)S(1)}, bf16[2,2,32,2048]{3,2,0,1:T(8,128)(2,1)S(1)}, u32[]{:S(2)}, u32[]{:S(2)}) collective-permute-start(bf16[2,2,32,2048]{3,2,0,1:T(8,128)(2,1)S(1)} %dynamic-slice_bitcast_fusion.9), channel_id=1, source_target_pairs={{0,4},{1,5},{2,6},{3,7},{4,0},{5,1},{6,2},{7,3},{8,12},{9,13},{10,... | collective-permute-start | bytes 1572872 | tf_op jit(solution)/shard_map/ppermute | solution.py:145
  606.8 32.2 %collective-permute-start.20 = (bf16[2,2,32,2048]{3,2,1,0:T(8,128)(2,1)S(1)}, bf16[2,2,32,2048]{3,2,1,0:T(8,128)(2,1)S(1)}, u32[]{:S(2)}, u32[]{:S(2)}) collective-permute-start(bf16[2,2,32,2048]{3,2,1,0:T(8,128)(2,1)S(1)} %dynamic-slice_bitcast_fusion.8), channel_id=1, source_target_pairs={{0,8},{1,9},{2,10},{3,11},{4,12},{5,13},{6,14},{7,15},{8,0},{9,1},... | collective-permute-start | bytes 1572872 | tf_op jit(solution)/shard_map/ppermute | solution.py:145
  617.0 24.8 %collective-permute-start.26 = (bf16[2,128,512]{2,1,0:T(8,128)(2,1)S(1)}, bf16[2,128,512]{2,1,0:T(8,128)(2,1)S(1)}, u32[]{:S(2)}, u32[]{:S(2)}) collective-permute-start(bf16[2,128,512]{2,1,0:T(8,128)(2,1)S(1)} %dynamic-slice_bitcast_fusion.14), channel_id=1, source_target_pairs={{0,8},{1,9},{2,10},{3,11},{4,12},{5,13},{6,14},{7,15},{8,0},{9,1},... | collective-permute-start | bytes 786440 | tf_op jit(solution)/shard_map/ppermute | solution.py:145
  621.3 21.0 %collective-permute-start.30 = (bf16[2,128,512]{2,1,0:T(8,128)(2,1)S(1)}, bf16[2,128,512]{2,1,0:T(8,128)(2,1)S(1)}, u32[]{:S(2)}, u32[]{:S(2)}) collective-permute-start(bf16[2,128,512]{2,1,0:T(8,128)(2,1)S(1)} %dynamic-slice_bitcast_fusion.13), channel_id=1, source_target_pairs={{0,16},{1,17},{2,18},{3,19},{4,20},{5,21},{6,22},{7,23},{8,24},{9,... | collective-permute-start | bytes 786440 | tf_op jit(solution)/shard_map/ppermute | solution.py:145
  624.8 22.1 %collective-permute-start.17 = (bf16[2,32,2048]{2,1,0:T(8,128)(2,1)S(1)}, bf16[2,32,2048]{2,1,0:T(8,128)(2,1)S(1)}, u32[]{:S(2)}, u32[]{:S(2)}) collective-permute-start(bf16[2,32,2048]{2,1,0:T(8,128)(2,1)S(1)} %dynamic-slice_bitcast_fusion.16), channel_id=1, source_target_pairs={{0,8},{1,9},{2,10},{3,11},{4,12},{5,13},{6,14},{7,15},{8,0},{9,1},... | collective-permute-start | bytes 786440 | tf_op jit(solution)/shard_map/ppermute | solution.py:145
  639.1 15.4 %collective-permute-start.21 = (bf16[2,32,2048]{2,1,0:T(8,128)(2,1)S(1)}, bf16[2,32,2048]{2,1,0:T(8,128)(2,1)S(1)}, u32[]{:S(2)}, u32[]{:S(2)}) collective-permute-start(bf16[2,32,2048]{2,1,0:T(8,128)(2,1)S(1)} %dynamic-slice_bitcast_fusion.15), channel_id=1, source_target_pairs={{0,16},{1,17},{2,18},{3,19},{4,20},{5,21},{6,22},{7,23},{8,24},{9,... | collective-permute-start | bytes 786440 | tf_op jit(solution)/shard_map/ppermute | solution.py:145
  641.9 15.5 %collective-permute-start.27 = (bf16[128,512]{1,0:T(8,128)(2,1)S(1)}, bf16[128,512]{1,0:T(8,128)(2,1)S(1)}, u32[]{:S(2)}, u32[]{:S(2)}) collective-permute-start(bf16[128,512]{1,0:T(8,128)(2,1)S(1)} %dynamic-slice_bitcast_fusion.21), channel_id=1, source_target_pairs={{0,16},{1,17},{2,18},{3,19},{4,20},{5,21},{6,22},{7,23},{8,24},{9,... | collective-permute-start | bytes 393224 | tf_op jit(solution)/shard_map/ppermute | solution.py:145
  642.4 15.1 %collective-permute-start.31 = (bf16[128,512]{1,0:T(8,128)(2,1)S(1)}, bf16[128,512]{1,0:T(8,128)(2,1)S(1)}, u32[]{:S(2)}, u32[]{:S(2)}) collective-permute-start(bf16[128,512]{1,0:T(8,128)(2,1)S(1)} %dynamic-slice_bitcast_fusion.20), channel_id=1, source_target_pairs={{0,2},{1,3},{2,0},{3,1},{4,6},{5,7},{6,4},{7,5},{8,10},{9,11},{10,... | collective-permute-start | bytes 393224 | tf_op jit(solution)/shard_map/ppermute | solution.py:145
  (26 other events, 189.4 us)
Sparse Core Ops, SparseCore 0:
  10.9 72.2 all-gather.6
  86.0 54.8 all-gather.8
  143.9 76.3 all-gather.10
  222.9 76.0 all-gather.12

commit v2 on v1

--- a/solution.py
+++ b/solution.py
@@ -276,6 +276,7 @@
 
     grad_attended = dot(grad_branch_one, whole_out, 1, 1).astype(BF16)
     grads = attention_call(attend_back_kernel, 3, labels, mixed_low, (grad_attended,))
+    grads, sum_down = lax.optimization_barrier((grads, sum_down))
     grad_mixed = jnp.concatenate(grads, axis=1)
     grad_query_bias = jnp.sum(grads[0].astype(F32), axis=0)
     grad_value_bias = jnp.sum(grads[2].astype(F32), axis=0)
@@ -302,6 +303,7 @@
         axis=1,
     )
     sum_small = scatter_sum(grad_small[:, None, :], (order_one,), device, count)[0]
+    grad_mixed, sum_up = lax.optimization_barrier((grad_mixed, sum_up))
     grad_tokens = grad_first_in + dot(grad_mixed, whole_qkv, 1, 1)
 
     shares = []

time: 678 us -> 711 us (1.049)
  waiting for transfers between devices: 256 us -> 279 us
  local copies, waits for them, and re-layouts: 53.4 us -> 60.6 us
    ppermute x37, waiting for transfers between devices: 101 us -> 125 us  [halve(): arrived = lax.ppermute(sent, 'dp', partners)]
  transfers between devices with their start and end apart: 41 -> 41, of which waited for: 23 -> 26; matrix products, arithmetic and copies ran while one was open for 16% -> 17% of each run, Pallas kernels for 10% -> 15%
where the time goes in v2:
time: 711 us; the launch traced here: 701 us
  waiting for transfers between devices  279 us (39%)
  matrix products  125 us (18%)
  Pallas kernels  107 us (15%)
  local copies, waits for them, and re-layouts  60.6 us (9%)
  blocking collectives  43.5 us (6%)
  other arithmetic  37.3 us (5%)
  starting transfers between devices  33.1 us (5%)
  between operations  15.1 us (2%)
    dot_general x11, matrix products, dot(): lax.dot_general(left, right, (((left_dim,), (right_dim,)), ((), ())), pre...  125 us
    ppermute x37, waiting for transfers between devices, halve(): arrived = lax.ppermute(sent, 'dp', partners)  125 us
    pallas_call x2, Pallas kernels, attention_call(): pl.pallas_call(kernel, grid=(micro_count, groups), in_specs=[pl.BlockSpec...  83.9 us
    all_gather x1, waiting for transfers between devices, body(): whole_up = lax.all_gather(up_weight, 'dp', axis=0, tiled=True)  70.5 us
    all_gather x1, waiting for transfers between devices, body(): whole_down = lax.all_gather(down_weight, 'dp', axis=0, tiled=True)  54 us
    all_gather x1, blocking collectives, body(): packed = lax.all_gather(jnp.concatenate(small), 'dp', axis=0, tiled=False)  43.5 us
    ppermute x37, starting transfers between devices, halve(): arrived = lax.ppermute(sent, 'dp', partners)  32.9 us
    pallas_call x1, Pallas kernels, up_call(): pl.pallas_call(up_kernel, grid=(units // block, 2), in_specs=[pl.BlockSpe...  23.2 us
  transfers between devices with their start and end apart: 41, of which 26 were waited for; matrix products, arithmetic and copies ran while one was open for 17% of the time, Pallas kernels for 15%

profile of v2, /device:TPU:0, one launch (start us, length us, event | category | flops | bytes accessed | tf_op | source)
XLA Modules:
  0.0 701.2 jit_solution(8812831181822293280)
XLA Ops:
  10.0 6.1 concatenate.40
  16.1 43.5 %all-gather.1 = bf16[32,1,384]{2,1,0:T(2,128)(2,1)S(1)} all-gather(bf16[1,1,384]{2,1,0:T(2,128)(2,1)S(1)} %reshape.294), channel_id=2, replica_groups=mesh['dp'=32] {'dp'}, dimensions={0}, use_global_device_ids=true | all-gather | bytes 25344 | tf_op jit(solution)/shard_map/all_gather | solution.py:209
  61.5 21.7 %all-gather.7.cloned.1.call-done = bf16[1024,3072]{1,0:T(8,128)(2,1)} async-done(((bf16[32,3072]{1,0:T(8,128)(2,1)}), bf16[1024,3072]{1,0:T(8,128)(2,1)}) %all-gather.7.cloned.1.call-update) | async-done | bytes 6291472 | tf_op jit(solution)/shard_map/all_gather | solution.py:210
  83.2 11.3 %add_convert_fusion.query_ref.key_ref.value_ref = bf16[1024,3072]{1,0:T(8,128)(2,1)} fusion(f32[3072]{0:T(1024)S(1)} %pad_maximum_fusion.3, bf16[1024,1024]{1,0:T(8,128)(2,1)} %param.16, bf16[1024,3072]{1,0:T(8,128)(2,1)} %all-gather.7.cloned.1.call-done), kind=kOutput, calls=%fused_computation.2 | convolution fusion | flops 6448742400 | bytes 14692352 | tf_op jit(solution)/shard_map/dot_general | solution.py:21
  94.5 40.4 %shard_map.271 = bf16[1024,1024]{1,0:T(8,128)(2,1)S(1)} custom-call(s32[1024,1]{1,0:T(8,128)S(1)} %bitcast.255, s32[2,1,512]{2,1,0:T(1,128)S(1)} %reshape.251.row_ref, bf16[1024,3072]{1,0:T(8,128)(2,1)} %add_convert_fusion.query_ref.key_ref.value_ref, bf16[1024,3072]{1,0:T(8,128)(2,1)} %add_convert_fusion.query_ref.key_ref.value_ref, ...), custom_call_target="tpu_custom_call" | custom-call | flops 2147483648 | bytes 8388608 | tf_op jit(solution)/shard_map/pallas_call | solution.py:85
  134.9 6.1 all-gather.9.cloned.1.call-done
  149.7 70.5 %all-gather.11.cloned.1.call-done.weight_ref = bf16[1024,4096]{1,0:T(8,128)(2,1)} async-done(((bf16[32,4096]{1,0:T(8,128)(2,1)}), bf16[1024,4096]{1,0:T(8,128)(2,1)}) %all-gather.11.cloned.1.call-update) | async-done | bytes 8388624 | tf_op jit(solution)/shard_map/all_gather | solution.py:212
  221.8 23.2 %shard_map.272 = (bf16[1024,4096]{1,0:T(8,128)(2,1)}, bf16[1024,4096]{1,0:T(8,128)(2,1)}) custom-call(bf16[1024,1024]{1,0:T(8,128)(2,1)S(1)} %copy-done, bf16[1024,4096]{1,0:T(8,128)(2,1)} %all-gather.11.cloned.1.call-done.weight_ref, f32[1,4096]{1,0:T(1,128)S(1)} %bitcast.257), custom_call_target="tpu_custom_call" | custom-call | flops 8589934592 | bytes 25165824 | tf_op jit(solution)/shard_map/pallas_call | solution.py:120
  245.0 54.0 %all-gather.13.cloned.1.call-done = bf16[4096,1024]{1,0:T(8,128)(2,1)} async-done(((bf16[128,1024]{1,0:T(8,128)(2,1)}), bf16[4096,1024]{1,0:T(8,128)(2,1)}) %all-gather.13.cloned.1.call-update) | async-done | bytes 8388624 | tf_op jit(solution)/shard_map/all_gather | solution.py:213
  299.0 15.0 %fusion.51 = (f32[1024]{0:T(1024)S(1)}, f32[1024,1024]{1,0:T(8,128)S(1)}) fusion(f32[1024]{0:T(1024)S(1)} %reshape.258, bf16[1024,4096]{1,0:T(8,128)(2,1)} %get-tuple-element.34, bf16[4096,1024]{1,0:T(8,128)(2,1)} %all-gather.13.cloned.1.call-done, f32[1024]{0:T(1024)S(1)} %reshape.256, f32[1024]{0:T(1024)S(1)} %reshape.255, ...), kind=kOutput, calls=%fused_computation.201 | convolution fusion | flops 8597273600 | bytes 25190400 | tf_op jit(solution)/shard_map/dot_general | solution.py:21
  322.3 11.3 %convolution_convert_fusion.1 = bf16[4096,1024]{1,0:T(8,128)(2,1)} fusion(bf16[1024,4096]{1,0:T(8,128)(2,1)S(1)} %bitcast.272, bf16[1024,1024]{1,0:T(8,128)(2,1)S(1)} %get-tuple-element.35), kind=kOutput, calls=%fused_computation.8 | convolution fusion | flops 8594128896 | bytes 18874368 | tf_op jit(solution)/shard_map/dot_general | solution.py:21
  333.7 16.7 %convert_reduce_fusion = (f32[4096]{0:T(1024)}, bf16[1024,4096]{1,0:T(8,128)(2,1)}) fusion(bf16[1024,4096]{1,0:T(8,128)(2,1)} %get-tuple-element.36, bf16[1024,1024]{1,0:T(8,128)(2,1)} %copy-done.10, bf16[4096,1024]{1,0:T(8,128)(2,1)} %all-gather.13.cloned.1.call-done), kind=kOutput, calls=%fused_computation | convolution fusion | flops 8610902016 | bytes 27279360 | tf_op jit(solution)/shard_map/dot_general | solution.py:21
  350.3 15.2 %convolution_convert_fusion = bf16[1024,4096]{1,0:T(8,128)(2,1)} fusion(bf16[1024,1024]{1,0:T(8,128)(2,1)} %fusion.10.hidden_ref, bf16[1024,4096]{1,0:T(8,128)(2,1)} %get-tuple-element.37), kind=kOutput, calls=%fused_computation.7 | convolution fusion | flops 8594128896 | bytes 18874368 | tf_op jit(solution)/shard_map/dot_general | solution.py:21
  365.6 19.5 %multiply_reduce_fusion = (f32[1024]{0:T(1024)S(1)}, f32[1024]{0:T(1024)S(1)}, f32[1024]{0:T(1024)S(1)}, f32[1024]{0:T(1024)S(1)}, f32[1024,1024]{1,0:T(8,128)}) fusion(f32[1024,1024]{1,0:T(8,128)} %copy-done.3, f32[1024]{0:T(1024)S(1)} %add_rsqrt_fusion.1, f32[1024]{0:T(1024)S(1)} %broadcast_multiply_fusion.5, f32[1024]{0:T(1024)S(1)} %reshape.255, ...), kind=kOutput, calls=%fused_computation.26 | convolution fusion | flops 8608804864 | bytes 31506432 | tf_op jit(solution)/shard_map/dot_general | solution.py:21
  385.1 5.7 convert_reduce_fusion.3
  394.8 6.9 constant_dynamic-slice_fusion.15
  406.6 6.3 constant_dynamic-slice_fusion.13
  421.1 6.2 collective-permute-done.29
  430.4 5.3 convolution_convert_fusion.2.grad_ref
  437.7 43.6 %shard_map.273 = (bf16[1024,1024]{1,0:T(8,128)(2,1)S(1)}, bf16[1024,1024]{1,0:T(8,128)(2,1)S(1)}, bf16[1024,1024]{1,0:T(8,128)(2,1)}) custom-call(s32[1024,1]{1,0:T(8,128)S(1)} %bitcast.256, s32[2,1,512]{2,1,0:T(1,128)S(1)} %reshape.251.row_ref, bf16[1024,3072]{1,0:T(8,128)(2,1)} %add_convert_fusion.query_ref.key_ref.value_ref, ...), custom_call_target="tpu_custom_call" | custom-call | flops 10737418240 | bytes 14680064 | tf_op jit(solution)/shard_map/pallas_call | solution.py:85
  487.3 5.6 fusion.1
  502.4 17.5 %collective-permute-done.1 = bf16[2,2,2,128,512]{4,3,0,1,2:T(8,128)(2,1)} collective-permute-done((bf16[2,2,2,128,512]{4,3,0,1,2:T(8,128)(2,1)S(1)}, bf16[2,2,2,128,512]{4,3,0,1,2:T(8,128)(2,1)}, u32[]{:S(2)}, u32[]{:S(2)}) %collective-permute-start.1) | collective-permute-done | bytes 1048608 | tf_op jit(solution)/shard_map/ppermute | solution.py:145
  522.7 16.1 %collective-permute-done.10 = bf16[2,2,2,32,2048]{4,3,0,1,2:T(8,128)(2,1)S(1)} collective-permute-done((bf16[2,2,2,32,2048]{4,3,0,1,2:T(8,128)(2,1)S(1)}, bf16[2,2,2,32,2048]{4,3,0,1,2:T(8,128)(2,1)S(1)}, u32[]{:S(2)}, u32[]{:S(2)}) %collective-permute-start.10) | collective-permute-done | bytes 1048608 | tf_op jit(solution)/shard_map/ppermute | solution.py:145
  543.6 10.5 %collective-permute-done.2 = bf16[2,2,128,512]{3,2,0,1:T(8,128)(2,1)S(1)} collective-permute-done((bf16[2,2,128,512]{3,2,0,1:T(8,128)(2,1)S(1)}, bf16[2,2,128,512]{3,2,0,1:T(8,128)(2,1)S(1)}, u32[]{:S(2)}, u32[]{:S(2)}) %collective-permute-start.2) | collective-permute-done | bytes 524320 | tf_op jit(solution)/shard_map/ppermute | solution.py:145
  574.9 9.2 %collective-permute-done.16 = bf16[2,32,2048]{2,1,0:T(8,128)(2,1)S(1)} collective-permute-done((bf16[2,32,2048]{2,1,0:T(8,128)(2,1)S(1)}, bf16[2,32,2048]{2,1,0:T(8,128)(2,1)S(1)}, u32[]{:S(2)}, u32[]{:S(2)}) %collective-permute-start.16) | collective-permute-done | bytes 262176 | tf_op jit(solution)/shard_map/ppermute | solution.py:145
  597.5 11.8 %convert_bitcast_fusion = bf16[1024,3072]{0,1:T(8,128)(2,1)} fusion(bf16[1024,3072]{1,0:T(8,128)(2,1)} %constant_dynamic-update-slice_fusion, bf16[1024,1024]{1,0:T(8,128)(2,1)S(1)} %copy-done.11), kind=kOutput, calls=%fused_computation.11 | convolution fusion | flops 6445596672 | bytes 14680064 | tf_op jit(solution)/shard_map/dot_general | solution.py:21
  609.3 8.6 %copy.91 = bf16[1024,3072]{1,0:T(8,128)(2,1)} copy(bf16[1024,3072]{0,1:T(8,128)(2,1)} %convert_bitcast_fusion) | data formatting | bytes 12582912 | tf_op jit(solution)/shard_map/optimization_barrier | solution.py:284
  628.4 11.8 %add_convert_fusion.1 = bf16[1024,1024]{1,0:T(8,128)(2,1)} fusion(f32[1024,1024]{1,0:T(8,128)S(1)} %copy-done.7, bf16[1024,3072]{1,0:T(8,128)(2,1)} %constant_dynamic-update-slice_fusion, bf16[1024,3072]{1,0:T(8,128)(2,1)} %all-gather.7.cloned.1.call-done), kind=kOutput, calls=%fused_computation.31 | convolution fusion | flops 6444548096 | bytes 18874368 | tf_op jit(solution)/shard_map/dot_general | solution.py:21
  647.9 13.4 %collective-permute-done.19 = bf16[2,2,2,32,1536]{4,3,0,1,2:T(8,128)(2,1)S(1)} collective-permute-done((bf16[2,2,2,32,1536]{4,3,0,1,2:T(8,128)(2,1)S(1)}, bf16[2,2,2,32,1536]{4,3,0,1,2:T(8,128)(2,1)S(1)}, u32[]{:S(2)}, u32[]{:S(2)}) %collective-permute-start.19) | collective-permute-done | bytes 786464 | tf_op jit(solution)/shard_map/ppermute | solution.py:145
  666.1 5.5 collective-permute-done.20
  672.1 5.6 collective-permute-done.24
  681.0 7.7 %collective-permute-done.25 = bf16[2,32,1536]{2,1,0:T(8,128)(2,1)S(1)} collective-permute-done((bf16[2,32,1536]{2,1,0:T(8,128)(2,1)S(1)}, bf16[2,32,1536]{2,1,0:T(8,128)(2,1)S(1)}, u32[]{:S(2)}, u32[]{:S(2)}) %collective-permute-start.25) | collective-permute-done | bytes 196640 | tf_op jit(solution)/shard_map/ppermute | solution.py:145
  (237 shorter events, 134.4 us)
Async XLA Ops:
  7.2 76.0 %all-gather.7.cloned.1.call-start = ((), (), s32[]{:S(2)}) async-start(), calls=%async_computation | async-start | bytes 6488064 | tf_op jit(solution)/shard_map/all_gather | solution.py:210
  7.9 133.1 %all-gather.9.cloned.1.call-start = ((), (), s32[]{:S(2)}) async-start(), calls=%async_computation.1 | async-start | bytes 2162688 | tf_op jit(solution)/shard_map/all_gather | solution.py:211
  8.7 211.5 %all-gather.11.cloned.1.call-start = ((), (), s32[]{:S(2)}) async-start(), calls=%async_computation.2 | async-start | bytes 8650752 | tf_op jit(solution)/shard_map/all_gather | solution.py:212
  9.4 289.6 %all-gather.13.cloned.1.call-start = ((), (), s32[]{:S(2)}) async-start(), calls=%async_computation.3 | async-start | bytes 8650752 | tf_op jit(solution)/shard_map/all_gather | solution.py:213
  404.4 83.0 %collective-permute-start = (bf16[2,2,2,2,128,1024]{5,4,3,0,1,2:T(8,128)(2,1)}, bf16[2,2,2,2,128,1024]{5,4,3,0,1,2:T(8,128)(2,1)}, u32[]{:S(2)}, u32[]{:S(2)}) collective-permute-start(bf16[2,2,2,2,128,1024]{5,4,3,0,1,2:T(8,128)(2,1)} %bitcast.251), channel_id=1, source_target_pairs={{0,1},{1,0},{2,3},{3,2},{4,5},{5,4},{6,7},{7,6},{8,9},{9,8},{10,11... | collective-permute-start | bytes 12582920 | tf_op jit(solution)/shard_map/ppermute | solution.py:145
  405.1 14.1 %collective-permute-start.28 = (bf16[2,2,2,32,1024]{4,3,2,0,1:T(8,128)(2,1)S(1)}, bf16[2,2,2,32,1024]{4,3,2,0,1:T(8,128)(2,1)S(1)}, u32[]{:S(2)}, u32[]{:S(2)}) collective-permute-start(bf16[2,2,2,32,1024]{4,3,2,0,1:T(8,128)(2,1)S(1)} %dynamic-slice_bitcast_fusion.6), channel_id=1, source_target_pairs={{0,4},{1,5},{2,6},{3,7},{4,0},{5,1},{6,2},{7,3},{8,12},{9,13},{10,... | collective-permute-start | bytes 1572872 | tf_op jit(solution)/shard_map/ppermute | solution.py:145
  415.2 80.6 %collective-permute-start.9 = (bf16[2,2,2,2,32,4096]{5,4,3,0,1,2:T(8,128)(2,1)}, bf16[2,2,2,2,32,4096]{5,4,3,0,1,2:T(8,128)(2,1)}, u32[]{:S(2)}, u32[]{:S(2)}) collective-permute-start(bf16[2,2,2,2,32,4096]{5,4,3,0,1,2:T(8,128)(2,1)} %bitcast.250), channel_id=1, source_target_pairs={{0,1},{1,0},{2,3},{3,2},{4,5},{5,4},{6,7},{7,6},{8,9},{9,8},{10,11... | collective-permute-start | bytes 12582920 | tf_op jit(solution)/shard_map/ppermute | solution.py:145
  436.1 50.5 %collective-permute-start.31 = (bf16[32,1024]{1,0:T(8,128)(2,1)S(1)}, bf16[32,1024]{1,0:T(8,128)(2,1)S(1)}, u32[]{:S(2)}, u32[]{:S(2)}) collective-permute-start(bf16[32,1024]{1,0:T(8,128)(2,1)S(1)} %dynamic-slice_bitcast_fusion.27), channel_id=1, source_target_pairs={{0,2},{1,3},{2,0},{3,1},{4,6},{5,7},{6,4},{7,5},{8,10},{9,11},{10,... | collective-permute-start | bytes 196616 | tf_op jit(solution)/shard_map/ppermute | solution.py:145
  493.6 26.3 %collective-permute-start.1 = (bf16[2,2,2,128,512]{4,3,0,1,2:T(8,128)(2,1)S(1)}, bf16[2,2,2,128,512]{4,3,0,1,2:T(8,128)(2,1)}, u32[]{:S(2)}, u32[]{:S(2)}) collective-permute-start(bf16[2,2,2,128,512]{4,3,0,1,2:T(8,128)(2,1)S(1)} %dynamic-slice_bitcast_fusion.4), channel_id=1, source_target_pairs={{0,2},{1,3},{2,0},{3,1},{4,6},{5,7},{6,4},{7,5},{8,10},{9,11},{10,... | collective-permute-start | bytes 3145736 | tf_op jit(solution)/shard_map/ppermute | solution.py:145
  494.3 27.8 %collective-permute-start.5 = (bf16[2,2,2,128,512]{4,3,2,0,1:T(8,128)(2,1)S(1)}, bf16[2,2,2,128,512]{4,3,2,0,1:T(8,128)(2,1)S(1)}, u32[]{:S(2)}, u32[]{:S(2)}) collective-permute-start(bf16[2,2,2,128,512]{4,3,2,0,1:T(8,128)(2,1)S(1)} %dynamic-slice_bitcast_fusion.3), channel_id=1, source_target_pairs={{0,4},{1,5},{2,6},{3,7},{4,0},{5,1},{6,2},{7,3},{8,12},{9,13},{10,... | collective-permute-start | bytes 3145736 | tf_op jit(solution)/shard_map/ppermute | solution.py:145
  500.2 38.6 %collective-permute-start.10 = (bf16[2,2,2,32,2048]{4,3,0,1,2:T(8,128)(2,1)S(1)}, bf16[2,2,2,32,2048]{4,3,0,1,2:T(8,128)(2,1)S(1)}, u32[]{:S(2)}, u32[]{:S(2)}) collective-permute-start(bf16[2,2,2,32,2048]{4,3,0,1,2:T(8,128)(2,1)S(1)} %dynamic-slice_bitcast_fusion.2), channel_id=1, source_target_pairs={{0,2},{1,3},{2,0},{3,1},{4,6},{5,7},{6,4},{7,5},{8,10},{9,11},{10,... | collective-permute-start | bytes 3145736 | tf_op jit(solution)/shard_map/ppermute | solution.py:145
  500.9 42.0 %collective-permute-start.14 = (bf16[2,2,2,32,2048]{4,3,2,0,1:T(8,128)(2,1)S(1)}, bf16[2,2,2,32,2048]{4,3,2,0,1:T(8,128)(2,1)S(1)}, u32[]{:S(2)}, u32[]{:S(2)}) collective-permute-start(bf16[2,2,2,32,2048]{4,3,2,0,1:T(8,128)(2,1)S(1)} %dynamic-slice_bitcast_fusion.1), channel_id=1, source_target_pairs={{0,4},{1,5},{2,6},{3,7},{4,0},{5,1},{6,2},{7,3},{8,12},{9,13},{10,... | collective-permute-start | bytes 3145736 | tf_op jit(solution)/shard_map/ppermute | solution.py:145
  521.5 32.7 %collective-permute-start.2 = (bf16[2,2,128,512]{3,2,0,1:T(8,128)(2,1)S(1)}, bf16[2,2,128,512]{3,2,0,1:T(8,128)(2,1)S(1)}, u32[]{:S(2)}, u32[]{:S(2)}) collective-permute-start(bf16[2,2,128,512]{3,2,0,1:T(8,128)(2,1)S(1)} %dynamic-slice_bitcast_fusion.10), channel_id=1, source_target_pairs={{0,4},{1,5},{2,6},{3,7},{4,0},{5,1},{6,2},{7,3},{8,12},{9,13},{10,... | collective-permute-start | bytes 1572872 | tf_op jit(solution)/shard_map/ppermute | solution.py:145
  522.5 32.1 %collective-permute-start.6 = (bf16[2,2,128,512]{3,2,1,0:T(8,128)(2,1)S(1)}, bf16[2,2,128,512]{3,2,1,0:T(8,128)(2,1)S(1)}, u32[]{:S(2)}, u32[]{:S(2)}) collective-permute-start(bf16[2,2,128,512]{3,2,1,0:T(8,128)(2,1)S(1)} %dynamic-slice_bitcast_fusion.9), channel_id=1, source_target_pairs={{0,8},{1,9},{2,10},{3,11},{4,12},{5,13},{6,14},{7,15},{8,0},{9,1},... | collective-permute-start | bytes 1572872 | tf_op jit(solution)/shard_map/ppermute | solution.py:145
  539.3 22.4 %collective-permute-start.11 = (bf16[2,2,32,2048]{3,2,0,1:T(8,128)(2,1)S(1)}, bf16[2,2,32,2048]{3,2,0,1:T(8,128)(2,1)S(1)}, u32[]{:S(2)}, u32[]{:S(2)}) collective-permute-start(bf16[2,2,32,2048]{3,2,0,1:T(8,128)(2,1)S(1)} %dynamic-slice_bitcast_fusion.8), channel_id=1, source_target_pairs={{0,4},{1,5},{2,6},{3,7},{4,0},{5,1},{6,2},{7,3},{8,12},{9,13},{10,... | collective-permute-start | bytes 1572872 | tf_op jit(solution)/shard_map/ppermute | solution.py:145
  543.4 19.1 %collective-permute-start.15 = (bf16[2,2,32,2048]{3,2,1,0:T(8,128)(2,1)S(1)}, bf16[2,2,32,2048]{3,2,1,0:T(8,128)(2,1)S(1)}, u32[]{:S(2)}, u32[]{:S(2)}) collective-permute-start(bf16[2,2,32,2048]{3,2,1,0:T(8,128)(2,1)S(1)} %dynamic-slice_bitcast_fusion.7), channel_id=1, source_target_pairs={{0,8},{1,9},{2,10},{3,11},{4,12},{5,13},{6,14},{7,15},{8,0},{9,1},... | collective-permute-start | bytes 1572872 | tf_op jit(solution)/shard_map/ppermute | solution.py:145
  554.4 14.0 %collective-permute-start.3 = (bf16[2,128,512]{2,1,0:T(8,128)(2,1)S(1)}, bf16[2,128,512]{2,1,0:T(8,128)(2,1)S(1)}, u32[]{:S(2)}, u32[]{:S(2)}) collective-permute-start(bf16[2,128,512]{2,1,0:T(8,128)(2,1)S(1)} %dynamic-slice_bitcast_fusion.17), channel_id=1, source_target_pairs={{0,8},{1,9},{2,10},{3,11},{4,12},{5,13},{6,14},{7,15},{8,0},{9,1},... | collective-permute-start | bytes 786440 | tf_op jit(solution)/shard_map/ppermute | solution.py:145
  554.8 13.8 %collective-permute-start.7 = (bf16[2,128,512]{2,1,0:T(8,128)(2,1)S(1)}, bf16[2,128,512]{2,1,0:T(8,128)(2,1)S(1)}, u32[]{:S(2)}, u32[]{:S(2)}) collective-permute-start(bf16[2,128,512]{2,1,0:T(8,128)(2,1)S(1)} %dynamic-slice_bitcast_fusion.16), channel_id=1, source_target_pairs={{0,16},{1,17},{2,18},{3,19},{4,20},{5,21},{6,22},{7,23},{8,24},{9,... | collective-permute-start | bytes 786440 | tf_op jit(solution)/shard_map/ppermute | solution.py:145
  561.9 12.3 %collective-permute-start.12 = (bf16[2,32,2048]{2,1,0:T(8,128)(2,1)S(1)}, bf16[2,32,2048]{2,1,0:T(8,128)(2,1)S(1)}, u32[]{:S(2)}, u32[]{:S(2)}) collective-permute-start(bf16[2,32,2048]{2,1,0:T(8,128)(2,1)S(1)} %dynamic-slice_bitcast_fusion.15), channel_id=1, source_target_pairs={{0,8},{1,9},{2,10},{3,11},{4,12},{5,13},{6,14},{7,15},{8,0},{9,1},... | collective-permute-start | bytes 786440 | tf_op jit(solution)/shard_map/ppermute | solution.py:145
  562.6 21.4 %collective-permute-start.16 = (bf16[2,32,2048]{2,1,0:T(8,128)(2,1)S(1)}, bf16[2,32,2048]{2,1,0:T(8,128)(2,1)S(1)}, u32[]{:S(2)}, u32[]{:S(2)}) collective-permute-start(bf16[2,32,2048]{2,1,0:T(8,128)(2,1)S(1)} %dynamic-slice_bitcast_fusion.14), channel_id=1, source_target_pairs={{0,16},{1,17},{2,18},{3,19},{4,20},{5,21},{6,22},{7,23},{8,24},{9,... | collective-permute-start | bytes 786440 | tf_op jit(solution)/shard_map/ppermute | solution.py:145
  568.5 17.6 %collective-permute-start.4 = (bf16[128,512]{1,0:T(8,128)(2,1)S(1)}, bf16[128,512]{1,0:T(8,128)(2,1)S(1)}, u32[]{:S(2)}, u32[]{:S(2)}) collective-permute-start(bf16[128,512]{1,0:T(8,128)(2,1)S(1)} %dynamic-slice_bitcast_fusion.24), channel_id=1, source_target_pairs={{0,16},{1,17},{2,18},{3,19},{4,20},{5,21},{6,22},{7,23},{8,24},{9,... | collective-permute-start | bytes 393224 | tf_op jit(solution)/shard_map/ppermute | solution.py:145
  568.7 17.5 %collective-permute-start.8 = (bf16[128,512]{1,0:T(8,128)(2,1)S(1)}, bf16[128,512]{1,0:T(8,128)(2,1)S(1)}, u32[]{:S(2)}, u32[]{:S(2)}) collective-permute-start(bf16[128,512]{1,0:T(8,128)(2,1)S(1)} %dynamic-slice_bitcast_fusion.23), channel_id=1, source_target_pairs={{0,2},{1,3},{2,0},{3,1},{4,6},{5,7},{6,4},{7,5},{8,10},{9,11},{10,... | collective-permute-start | bytes 393224 | tf_op jit(solution)/shard_map/ppermute | solution.py:145
  574.9 45.8 %collective-permute-start.13 = (bf16[32,2048]{1,0:T(8,128)(2,1)}, bf16[32,2048]{1,0:T(8,128)(2,1)S(1)}, u32[]{:S(2)}, u32[]{:S(2)}) collective-permute-start(bf16[32,2048]{1,0:T(8,128)(2,1)} %dynamic-slice_bitcast_fusion.22), channel_id=1, source_target_pairs={{0,16},{1,17},{2,18},{3,19},{4,20},{5,21},{6,22},{7,23},{8,24},{9,... | collective-permute-start | bytes 393224 | tf_op jit(solution)/shard_map/ppermute | solution.py:145
  584.2 38.1 %collective-permute-start.17 = (bf16[32,2048]{1,0:T(8,128)(2,1)S(1)}, bf16[32,2048]{1,0:T(8,128)(2,1)S(1)}, u32[]{:S(2)}, u32[]{:S(2)}) collective-permute-start(bf16[32,2048]{1,0:T(8,128)(2,1)S(1)} %dynamic-slice_bitcast_fusion.21), channel_id=1, source_target_pairs={{0,2},{1,3},{2,0},{3,1},{4,6},{5,7},{6,4},{7,5},{8,10},{9,11},{10,... | collective-permute-start | bytes 393224 | tf_op jit(solution)/shard_map/ppermute | solution.py:145
  592.4 28.3 %collective-permute-start.32 = (f32[2,2,2,2,1,384]{5,4,3,2,1,0:T(1,128)S(1)}, f32[2,2,2,2,1,384]{5,4,3,2,1,0:T(1,128)S(1)}, u32[]{:S(2)}, u32[]{:S(2)}) collective-permute-start(f32[2,2,2,2,1,384]{5,4,3,2,1,0:T(1,128)S(1)} %dynamic-slice_bitcast_fusion.28), channel_id=1, source_target_pairs={{0,1},{1,0},{2,3},{3,2},{4,5},{5,4},{6,7},{7,6},{8,9},{9,8},{10,11... | collective-permute-start | bytes 73736 | tf_op jit(solution)/shard_map/ppermute | solution.py:145
  620.2 22.5 %collective-permute-start.18 = (bf16[2,2,2,2,32,3072]{5,4,3,2,1,0:T(8,128)(2,1)S(1)}, bf16[2,2,2,2,32,3072]{5,4,3,2,1,0:T(8,128)(2,1)S(1)}, u32[]{:S(2)}, u32[]{:S(2)}) collective-permute-start(bf16[2,2,2,2,32,3072]{5,4,3,2,1,0:T(8,128)(2,1)S(1)} %dynamic-slice_bitcast_fusion), channel_id=1, source_target_pairs={{0,1},{1,0},{2,3},{3,2},{4,5},{5,4},{6,7},{7,6},{8,9},{9,8},{10,11... | collective-permute-start | bytes 9437192 | tf_op jit(solution)/shard_map/ppermute | solution.py:145
  628.3 11.9 %collective-permute-start.35 = (f32[2,1,384]{2,1,0:T(1,128)S(1)}, f32[2,1,384]{2,1,0:T(1,128)S(1)}, u32[]{:S(2)}, u32[]{:S(2)}) collective-permute-start(f32[2,1,384]{2,1,0:T(1,128)S(1)} %fusion.41), channel_id=1, source_target_pairs={{0,8},{1,9},{2,10},{3,11},{4,12},{5,13},{6,14},{7,15},{8,0},{9,1},... | collective-permute-start | bytes 9224 | tf_op jit(solution)/shard_map/ppermute | solution.py:145
  644.5 16.8 %collective-permute-start.19 = (bf16[2,2,2,32,1536]{4,3,0,1,2:T(8,128)(2,1)S(1)}, bf16[2,2,2,32,1536]{4,3,0,1,2:T(8,128)(2,1)S(1)}, u32[]{:S(2)}, u32[]{:S(2)}) collective-permute-start(bf16[2,2,2,32,1536]{4,3,0,1,2:T(8,128)(2,1)S(1)} %bitcast.265), channel_id=1, source_target_pairs={{0,2},{1,3},{2,0},{3,1},{4,6},{5,7},{6,4},{7,5},{8,10},{9,11},{10,... | collective-permute-start | bytes 2359304 | tf_op jit(solution)/shard_map/ppermute | solution.py:145
  646.7 19.1 %collective-permute-start.23 = (bf16[2,2,2,32,1536]{4,3,2,1,0:T(8,128)(2,1)S(1)}, bf16[2,2,2,32,1536]{4,3,2,1,0:T(8,128)(2,1)S(1)}, u32[]{:S(2)}, u32[]{:S(2)}) collective-permute-start(bf16[2,2,2,32,1536]{4,3,2,1,0:T(8,128)(2,1)S(1)} %dynamic-slice_bitcast_fusion.5), channel_id=1, source_target_pairs={{0,4},{1,5},{2,6},{3,7},{4,0},{5,1},{6,2},{7,3},{8,12},{9,13},{10,... | collective-permute-start | bytes 2359304 | tf_op jit(solution)/shard_map/ppermute | solution.py:145
  661.5 10.1 %collective-permute-start.20 = (bf16[2,2,32,1536]{3,2,0,1:T(8,128)(2,1)S(1)}, bf16[2,2,32,1536]{3,2,0,1:T(8,128)(2,1)S(1)}, u32[]{:S(2)}, u32[]{:S(2)}) collective-permute-start(bf16[2,2,32,1536]{3,2,0,1:T(8,128)(2,1)S(1)} %dynamic-slice_bitcast_fusion.12), channel_id=1, source_target_pairs={{0,4},{1,5},{2,6},{3,7},{4,0},{5,1},{6,2},{7,3},{8,12},{9,13},{10,... | collective-permute-start | bytes 1179656 | tf_op jit(solution)/shard_map/ppermute | solution.py:145
  666.0 11.8 %collective-permute-start.24 = (bf16[2,2,32,1536]{3,2,1,0:T(8,128)(2,1)S(1)}, bf16[2,2,32,1536]{3,2,1,0:T(8,128)(2,1)S(1)}, u32[]{:S(2)}, u32[]{:S(2)}) collective-permute-start(bf16[2,2,32,1536]{3,2,1,0:T(8,128)(2,1)S(1)} %dynamic-slice_bitcast_fusion.11), channel_id=1, source_target_pairs={{0,8},{1,9},{2,10},{3,11},{4,12},{5,13},{6,14},{7,15},{8,0},{9,1},... | collective-permute-start | bytes 1179656 | tf_op jit(solution)/shard_map/ppermute | solution.py:145
  677.9 10.8 %collective-permute-start.25 = (bf16[2,32,1536]{2,1,0:T(8,128)(2,1)S(1)}, bf16[2,32,1536]{2,1,0:T(8,128)(2,1)S(1)}, u32[]{:S(2)}, u32[]{:S(2)}) collective-permute-start(bf16[2,32,1536]{2,1,0:T(8,128)(2,1)S(1)} %dynamic-slice_bitcast_fusion.18), channel_id=1, source_target_pairs={{0,16},{1,17},{2,18},{3,19},{4,20},{5,21},{6,22},{7,23},{8,24},{9,... | collective-permute-start | bytes 589832 | tf_op jit(solution)/shard_map/ppermute | solution.py:145
  (25 other events, 170.0 us)
Sparse Core Ops, SparseCore 0:
  10.9 72.2 all-gather.6
  86.0 54.8 all-gather.8
  143.8 76.2 all-gather.10
  222.9 76.0 all-gather.12
